TPU v7x, 32 devices: a whole 2x2x4 slice. The times are simulated.
32 devices in a mesh: dp: 2 (over core), seq: 4 (over z), tensor: 4 (over y, x).
Axes of the slice: x: 2, y: 2, z: 4, core: 2. Of those that a mesh axis runs over, the one named last changes fastest.
Arguments:
- tokens: bfloat16 [2, 2048, 1024], P('dp', 'seq'), may hold values from -6 to 6
- cotangent: bfloat16 [2, 2048, 1024], P('dp', 'seq'), may hold values from -6 to 6
- attention_gain: bfloat16 [1024], replicated, may hold values from 0.5 to 1.5
- query_proj: bfloat16 [1024, 512], P(None, 'tensor'), may hold values from -0.1875 to 0.1875
- key_proj: bfloat16 [1024, 512], P(None, 'tensor'), may hold values from -0.1875 to 0.1875
- value_proj: bfloat16 [1024, 1024], P(None, 'tensor'), may hold values from -0.1875 to 0.1875
- query_conv: bfloat16 [4, 512], P(None, 'tensor'), may hold values from -3 to 3
- key_conv: bfloat16 [4, 512], P(None, 'tensor'), may hold values from -3 to 3
- value_conv: bfloat16 [4, 1024], P(None, 'tensor'), may hold values from -3 to 3
- decay_down: bfloat16 [1024, 16], replicated, may hold values from -0.1875 to 0.1875
- decay_up: bfloat16 [16, 512], P(None, 'tensor'), may hold values from -2 to 2
- decay_bias: float32 [512], P('tensor'), may hold values from 0.3 to 10
- swish_proj: bfloat16 [1024, 1024], P(None, 'tensor'), may hold values from -0.1875 to 0.1875
- head_gain: bfloat16 [256], replicated, may hold values from 0.5 to 1.5
- output_proj: bfloat16 [1024, 1024], P('tensor'), may hold values from -0.25 to 0.25
- feed_gain: bfloat16 [1024], replicated, may hold values from 0.5 to 1.5
- feed_gate: bfloat16 [1024, 2816], P(None, 'tensor'), may hold values from -0.1875 to 0.1875
- feed_lift: bfloat16 [1024, 2816], P(None, 'tensor'), may hold values from -0.1875 to 0.1875
- feed_down: bfloat16 [2816, 1024], P('tensor'), may hold values from -0.21875 to 0.21875
Outputs:
- mixed: bfloat16 [2, 2048, 1024], P('dp', 'seq')
- tokens_grad: float32 [2, 2048, 1024], P('dp', 'seq')
- grad_attention_gain: float32 [1024], replicated
- grad_query_proj: float32 [1024, 512], P(None, 'tensor')
- grad_key_proj: float32 [1024, 512], P(None, 'tensor')
- grad_value_proj: float32 [1024, 1024], P(None, 'tensor')
- grad_query_conv: float32 [4, 512], P(None, 'tensor')
- grad_key_conv: float32 [4, 512], P(None, 'tensor')
- grad_value_conv: float32 [4, 1024], P(None, 'tensor')
- grad_decay_down: float32 [1024, 16], replicated
- grad_decay_up: float32 [16, 512], P(None, 'tensor')
- grad_decay_bias: float32 [512], P('tensor')
- grad_swish_proj: float32 [1024, 1024], P(None, 'tensor')
- grad_head_gain: float32 [256], replicated
- grad_output_proj: float32 [1024, 1024], P('tensor')
- grad_feed_gain: float32 [1024], replicated
- grad_feed_gate: float32 [1024, 2816], P(None, 'tensor')
- grad_feed_lift: float32 [1024, 2816], P(None, 'tensor')
- grad_feed_down: float32 [2816, 1024], P('tensor')
All inputs are finite; a program needn't handle non-finite values.
Results may differ from a plain program's by a relative error of at most 0.017.
The roundings to bfloat16 on the way count: a program that leaves them out, or rounds other values in their place, can miss the bound.
Values may be sent and summed in bfloat16 or wider, within the bound.
A program may use at most 128 MiB of HBM per device.

v0:
```python
import jax
import jax.numpy as jnp
from jax import lax
from jax.sharding import PartitionSpec as P

HEAD_KEY = 128
SPAN = 64


highest = lax.Precision.HIGHEST
epsilon = 1e-06


def shifted(x, axis, by):
    size = lax.axis_size(axis)
    pairs = [(i, i + by) for i in range(size) if 0 <= i + by < size]
    return lax.ppermute(x, axis, pairs)


def root_norm(values, gain):
    return values * lax.rsqrt(jnp.mean(values * values, axis=-1, keepdims=True) + epsilon) * gain


def convolve(padded, weight):
    width = weight.shape[0]
    length = padded.shape[1] - width + 1
    total = weight[0] * padded[:, 0:length]
    for offset in range(1, width):
        total = total + weight[offset] * padded[:, offset : offset + length]
    return jax.nn.silu(total)


def block_step(memory, block):
    queries, keylist, values, decays = block
    extent = queries.shape[1]
    cumul = jnp.cumsum(decays, axis=1)
    causal = (jnp.arange(extent)[:, None] >= jnp.arange(extent)[None, :])[None, :, :, None]
    spread = cumul[:, :, None, :] - cumul[:, None, :, :]
    weights = jnp.where(causal, jnp.exp(jnp.where(causal, spread, 0.0)), 0.0)
    scores = jnp.einsum("ntd,nsd,ntsd->nts", queries, keylist, weights, precision=highest)
    inner = jnp.einsum("nts,nse->nte", scores, values, precision=highest)
    carried = jnp.einsum("ntd,nde->nte", queries * jnp.exp(cumul), memory, precision=highest)
    ending = cumul[:, -1:, :]
    fresh = jnp.einsum("nsd,nse->nde", keylist * jnp.exp(ending - cumul), values, precision=highest)
    return (jnp.exp(ending[:, 0, :])[:, :, None] * memory + fresh, inner + carried)


def recurrence(queries, keylist, values, decays, memory):
    groups, length, _ = queries.shape
    blocks = length // SPAN

    def split_blocks(array):
        return jnp.moveaxis(array.reshape(groups, blocks, SPAN, array.shape[-1]), 1, 0)

    memory, outputs = lax.scan(
        jax.checkpoint(block_step),
        memory,
        (split_blocks(queries), split_blocks(keylist), split_blocks(values), split_blocks(decays)),
    )
    return (jnp.moveaxis(outputs, 0, 1).reshape(groups, length, -1), memory)


def to_heads(array, width):
    batch, length, channels = array.shape
    return (
        array.reshape(batch, length, channels // width, width)
        .transpose(0, 2, 1, 3)
        .reshape(batch * (channels // width), length, width)
    )


def from_heads(array, batch):
    groups, length, width = array.shape
    return (
        array.reshape(batch, groups // batch, length, width)
        .transpose(0, 2, 1, 3)
        .reshape(batch, length, groups // batch * width)
    )


def head_piece(outputs, gate, gain):
    return root_norm(outputs, gain) * jax.nn.silu(gate)


def feed_piece(gate_pre, lift_pre):
    return jax.nn.silu(gate_pre) * lift_pre


def on_device(
    tokens,
    cotangent,
    attention_gain,
    query_proj,
    key_proj,
    value_proj,
    query_conv,
    key_conv,
    value_conv,
    decay_down,
    decay_up,
    decay_bias,
    swish_proj,
    head_gain,
    output_proj,
    feed_gain,
    feed_gate,
    feed_lift,
    feed_down,
):
    batch, seglen, width = tokens.shape
    rows = batch * seglen
    key_width = query_proj.shape[1]
    value_width = value_proj.shape[1]
    head_value = head_gain.shape[0]
    conv_width = query_conv.shape[0]
    scale = HEAD_KEY ** (-0.5)
    inputs_flat = tokens.astype(jnp.float32).reshape(rows, width)
    attention_gain_f = attention_gain.astype(jnp.float32)
    feed_gain_f = feed_gain.astype(jnp.float32)
    hidden_f, norm_back = jax.vjp(root_norm, inputs_flat, attention_gain_f)
    hidden = hidden_f.astype(jnp.bfloat16)
    query_raw = jnp.dot(hidden, query_proj, preferred_element_type=jnp.float32).astype(jnp.bfloat16)
    key_raw = jnp.dot(hidden, key_proj, preferred_element_type=jnp.float32).astype(jnp.bfloat16)
    value_raw = jnp.dot(hidden, value_proj, preferred_element_type=jnp.float32).astype(jnp.bfloat16)
    raw_rows = jnp.concatenate([query_raw, key_raw, value_raw], 1).reshape(batch, seglen, -1)
    edge_rows = shifted(raw_rows[:, seglen - conv_width + 1 :], "seq", 1)
    padded = jnp.concatenate([edge_rows, raw_rows], 1).astype(jnp.float32)
    conv_all = jnp.concatenate([query_conv, key_conv, value_conv], 1).astype(jnp.float32)
    activated, conv_back = jax.vjp(convolve, padded, conv_all)
    queries = to_heads(activated[..., :key_width] * scale, HEAD_KEY)
    keylist = to_heads(activated[..., key_width : 2 * key_width], HEAD_KEY)
    values = to_heads(activated[..., 2 * key_width :], head_value)
    low_rank = jnp.dot(hidden, decay_down, preferred_element_type=jnp.float32)
    decay_logit = jnp.dot(low_rank, decay_up.astype(jnp.float32), precision=highest) + decay_bias
    log_decay = jax.nn.log_sigmoid(decay_logit) / 16.0
    decays = to_heads(log_decay.reshape(batch, seglen, key_width), HEAD_KEY)
    zero_state = jnp.zeros((queries.shape[0], HEAD_KEY, head_value), jnp.float32)
    local_out, local_state = recurrence(queries, keylist, values, decays, zero_state)
    cumul = jnp.cumsum(decays, axis=1)
    total = jnp.exp(cumul[:, -1])
    decayed_q = queries * jnp.exp(cumul)

    def forward_turn(turn, carry):
        received = shifted(carry[1], "seq", 1)
        return (received, total[:, :, None] * received + local_state)

    incoming, _ = lax.fori_loop(
        0, lax.axis_size("seq") - 1, forward_turn, (zero_state, local_state)
    )
    recurrent = local_out + jnp.einsum("ntd,nde->nte", decayed_q, incoming, precision=highest)
    recurrent = from_heads(recurrent, batch).reshape(batch, seglen, -1, head_value)
    swish_gate = jnp.dot(hidden, swish_proj, preferred_element_type=jnp.float32).reshape(
        batch, seglen, -1, head_value
    )
    gated_f, head_back = jax.vjp(head_piece, recurrent, swish_gate, head_gain.astype(jnp.float32))
    gated = gated_f.astype(jnp.bfloat16).reshape(rows, value_width)
    mixer_part = jnp.dot(gated, output_proj, preferred_element_type=jnp.float32)
    middle_own = inputs_flat + lax.psum(mixer_part, "tensor")
    hidden_two_own, norm_two_back = jax.vjp(root_norm, middle_own, feed_gain_f)
    hidden_two = hidden_two_own.astype(jnp.bfloat16)
    gate_pre = jnp.dot(hidden_two, feed_gate, preferred_element_type=jnp.float32)
    lift_pre = jnp.dot(hidden_two, feed_lift, preferred_element_type=jnp.float32)
    activation_f, feed_back = jax.vjp(feed_piece, gate_pre, lift_pre)
    activation = activation_f.astype(jnp.bfloat16)
    feed_part = jnp.dot(activation, feed_down, preferred_element_type=jnp.float32)
    mixed = (
        middle_own + lax.psum(feed_part.astype(jnp.bfloat16), "tensor").astype(jnp.float32)
    ).astype(jnp.bfloat16)
    mixed = mixed.reshape(batch, seglen, width)
    upstream = cotangent.astype(jnp.float32).reshape(rows, width)
    feed_out_grad = cotangent.reshape(rows, width)
    grad_feed_down = jnp.dot(activation.T, feed_out_grad, preferred_element_type=jnp.float32)
    activation_grad = jnp.dot(feed_out_grad, feed_down.T, preferred_element_type=jnp.float32)
    gate_pre_grad, lift_pre_grad = feed_back(activation_grad)
    gate_pre_grad = gate_pre_grad.astype(jnp.bfloat16)
    lift_pre_grad = lift_pre_grad.astype(jnp.bfloat16)
    grad_feed_gate = jnp.dot(hidden_two.T, gate_pre_grad, preferred_element_type=jnp.float32)
    grad_feed_lift = jnp.dot(hidden_two.T, lift_pre_grad, preferred_element_type=jnp.float32)
    hidden_two_part = jnp.dot(
        gate_pre_grad, feed_gate.T, preferred_element_type=jnp.float32
    ) + jnp.dot(lift_pre_grad, feed_lift.T, preferred_element_type=jnp.float32)
    two_grad_own = lax.psum(hidden_two_part, "tensor")
    middle_norm_grad, grad_feed_gain = norm_two_back(two_grad_own)
    middle_grad_own = upstream + middle_norm_grad
    mixer_grad = middle_grad_own.astype(jnp.bfloat16)
    grad_output_proj = jnp.dot(gated.T, mixer_grad, preferred_element_type=jnp.float32)
    gated_grad = jnp.dot(mixer_grad, output_proj.T, preferred_element_type=jnp.float32).reshape(
        batch, seglen, -1, head_value
    )
    recurrent_grad, swish_grad, head_gain_part = head_back(gated_grad)
    swish_gate_grad = swish_grad.reshape(rows, value_width).astype(jnp.bfloat16)
    recurrent_grad = to_heads(recurrent_grad.reshape(batch, seglen, value_width), head_value)
    local_pull = jnp.einsum("ntd,nte->nde", decayed_q, recurrent_grad, precision=highest)

    def backward_turn(turn, carry):
        received = shifted(carry[1].astype(jnp.bfloat16), "seq", -1).astype(jnp.float32)
        return (received, total[:, :, None] * received + local_pull)

    outgoing_grad, _ = lax.fori_loop(
        0, lax.axis_size("seq") - 1, backward_turn, (zero_state, local_pull)
    )
    _, recurrence_back = jax.vjp(recurrence, queries, keylist, values, decays, incoming)
    queries_grad, keys_grad, values_grad, decays_grad, _ = recurrence_back(
        (recurrent_grad, outgoing_grad)
    )
    activated_grad = jnp.concatenate(
        [
            from_heads(queries_grad, batch) * scale,
            from_heads(keys_grad, batch),
            from_heads(values_grad, batch),
        ],
        -1,
    )
    log_decay_grad = from_heads(decays_grad, batch).reshape(rows, key_width)
    logit_grad = log_decay_grad * jax.nn.sigmoid(-decay_logit) / 16.0
    grad_decay_bias = jnp.sum(logit_grad, axis=0)
    grad_decay_up = jnp.dot(low_rank.T, logit_grad, precision=highest)
    low_rank_part = jnp.dot(logit_grad, decay_up.astype(jnp.float32).T, precision=highest)
    padded_grad, conv_grad = conv_back(activated_grad)
    returned = shifted(padded_grad[:, : conv_width - 1], "seq", -1)
    raw_grad = padded_grad[:, conv_width - 1 :]
    raw_grad = jnp.concatenate(
        [raw_grad[:, : seglen - conv_width + 1], raw_grad[:, seglen - conv_width + 1 :] + returned],
        1,
    )
    raw_grad = raw_grad.astype(jnp.bfloat16).reshape(rows, -1)
    query_grad_raw = raw_grad[:, :key_width]
    key_grad_raw = raw_grad[:, key_width : 2 * key_width]
    value_grad_raw = raw_grad[:, 2 * key_width :]
    grad_query_proj = jnp.dot(hidden.T, query_grad_raw, preferred_element_type=jnp.float32)
    grad_key_proj = jnp.dot(hidden.T, key_grad_raw, preferred_element_type=jnp.float32)
    grad_value_proj = jnp.dot(hidden.T, value_grad_raw, preferred_element_type=jnp.float32)
    grad_swish_proj = jnp.dot(hidden.T, swish_gate_grad, preferred_element_type=jnp.float32)
    hidden_part = (
        jnp.dot(query_grad_raw, query_proj.T, preferred_element_type=jnp.float32)
        + jnp.dot(key_grad_raw, key_proj.T, preferred_element_type=jnp.float32)
        + jnp.dot(value_grad_raw, value_proj.T, preferred_element_type=jnp.float32)
        + jnp.dot(swish_gate_grad, swish_proj.T, preferred_element_type=jnp.float32)
    )
    decay_down_f = decay_down.astype(jnp.float32)
    hidden_sum, low_rank_grad, grad_head_gain = (
        lax.psum(hidden_part.astype(jnp.bfloat16), "tensor").astype(jnp.float32),
        lax.psum(low_rank_part.astype(jnp.bfloat16), "tensor").astype(jnp.float32),
        lax.psum(head_gain_part.astype(jnp.bfloat16), "tensor").astype(jnp.float32),
    )
    hidden_grad = hidden_sum + jnp.dot(low_rank_grad, decay_down_f.T, precision=highest)
    grad_decay_down = jnp.dot(hidden.astype(jnp.float32).T, low_rank_grad, precision=highest)
    inputs_norm_grad, grad_attention_gain = norm_back(hidden_grad)
    tokens_grad = middle_grad_own + inputs_norm_grad
    tokens_grad = tokens_grad.reshape(batch, seglen, width)
    grad_query_conv = conv_grad[:, :key_width]
    grad_key_conv = conv_grad[:, key_width : 2 * key_width]
    grad_value_conv = conv_grad[:, 2 * key_width :]
    (
        grad_attention_gain,
        grad_query_proj,
        grad_key_proj,
        grad_value_proj,
        grad_query_conv,
        grad_key_conv,
        grad_value_conv,
        grad_decay_down,
        grad_decay_up,
        grad_decay_bias,
        grad_swish_proj,
        grad_head_gain,
        grad_output_proj,
        grad_feed_gain,
        grad_feed_gate,
        grad_feed_lift,
        grad_feed_down,
    ) = lax.psum(
        (
            grad_attention_gain,
            grad_query_proj,
            grad_key_proj,
            grad_value_proj,
            grad_query_conv,
            grad_key_conv,
            grad_value_conv,
            grad_decay_down,
            grad_decay_up,
            grad_decay_bias,
            grad_swish_proj,
            grad_head_gain,
            grad_output_proj,
            grad_feed_gain,
            grad_feed_gate,
            grad_feed_lift,
            grad_feed_down,
        ),
        ("dp", "seq"),
    )
    return (
        mixed,
        tokens_grad,
        grad_attention_gain,
        grad_query_proj,
        grad_key_proj,
        grad_value_proj,
        grad_query_conv,
        grad_key_conv,
        grad_value_conv,
        grad_decay_down,
        grad_decay_up,
        grad_decay_bias,
        grad_swish_proj,
        grad_head_gain,
        grad_output_proj,
        grad_feed_gain,
        grad_feed_gate,
        grad_feed_lift,
        grad_feed_down,
    )


def solution(mesh):
    return jax.shard_map(
        on_device,
        mesh=mesh,
        in_specs=(
            P("dp", "seq", None),
            P("dp", "seq", None),
            P(),
            P(None, "tensor"),
            P(None, "tensor"),
            P(None, "tensor"),
            P(None, "tensor"),
            P(None, "tensor"),
            P(None, "tensor"),
            P(),
            P(None, "tensor"),
            P("tensor"),
            P(None, "tensor"),
            P(),
            P("tensor", None),
            P(),
            P(None, "tensor"),
            P(None, "tensor"),
            P("tensor", None),
        ),
        out_specs=(
            P("dp", "seq", None),
            P("dp", "seq", None),
            P(),
            P(None, "tensor"),
            P(None, "tensor"),
            P(None, "tensor"),
            P(None, "tensor"),
            P(None, "tensor"),
            P(None, "tensor"),
            P(),
            P(None, "tensor"),
            P("tensor"),
            P(None, "tensor"),
            P(),
            P("tensor", None),
            P(),
            P(None, "tensor"),
            P(None, "tensor"),
            P("tensor", None),
        ),
        check_vma=False,
    )
```

profile of v0, /device:TPU:0, one launch (start us, length us, event | category | flops | bytes accessed | tf_op | source)
XLA Modules:
  0.0 790.8 jit_solution(15070296040000256144)
XLA Ops:
  13.5 5.6 collective-permute-start.2
  31.2 2.9 fusion.111
  40.1 50.1 %while.75 = (s32[]{:T(128)}, f32[1,128,256]{2,1,0:T(8,128)S(1)}, f32[8,1,64,256]{3,2,1,0:T(8,128)}, f32[8,1,64,128]{3,2,1,0:T(8,128)}, f32[8,1,64,128]{3,2,1,0:T...) while((s32[]{:T(128)}, f32[1,128,256]{2,1,0:T(8,128)S(1)}, ...), condition=%wide.region_3.4_spmd.clone, body=%wide.region_1.3_spmd.clone.sunk | while | flops 66748416 | bytes 5470342 | solution.py:55
  91.0 21.0 %while.71 = (s32[]{:T(128)}, f32[1,128,256]{2,1,0:T(8,128)}, f32[1,128,256]{2,1,0:T(8,128)S(1)}, f32[1,128]{1,0:T(1,128)S(1)}, f32[1,128,256]{2,1,0:T(8,128)S(1)}, /*index=5*/s32[]{:T(128)}) while((s32[]{:T(128)}, f32[1,128,256]{2,1,0:T(8,128)}, f32[1,128,256]{2,1,0:T(8,128)S(1)}, f32[1,128]{1,0:T(1,128)S(1)}, f32[1,128,256]{2,1,0:T(8,128)S(1)}, ...), condition=%wide.region_7.8_spmd, body=%wide.region_6.7_spmd.sunk | while | flops 65538 | bytes 1442441 | solution.py:147
  91.0 2.8 collective-permute-start
  93.8 2.5 collective-permute-done
  97.0 4.3 collective-permute-start
  101.3 2.5 collective-permute-done
  104.5 4.3 collective-permute-start
  108.8 2.5 collective-permute-done
  112.0 1.9 multiply_reduce_fusion.10
  114.0 2.5 multiply_convert_fusion.3
  119.9 70.0 %all-reduce.18.cloned.1.call-done = f32[512,1024]{1,0:T(8,128)} async-done(((f32[512,1024]{1,0:T(8,128)}), f32[512,1024]{1,0:T(8,128)}) %all-reduce.18.cloned.1.call-update) | async-done | bytes 2097168 | tf_op jit(solution)/shard_map/psum | solution.py:158
  189.9 1.9 multiply_reduce_fusion.3
  199.5 2.3 convolution_add_fusion.2
  202.8 22.4 %while.73 = (s32[]{:T(128)}, f32[1,128,256]{2,1,0:T(8,128)S(1)}, f32[8,1,128,256]{3,2,1,0:T(8,128)}, f32[8,1,64,128]{3,2,1,0:T(8,128)}, f32[8,1,64,128]{3,2,1,0:...) while((s32[]{:T(128)}, f32[1,128,256]{2,1,0:T(8,128)S(1)}, f32[8,1,128,256]{3,2,1,0:T(8,128)}, ...), condition=%wide.region_19.20_spmd, body=%wide.region_17.19_spmd.sunk | while | flops 25763840 | bytes 790633 | solution.py:55
  225.2 2.0 convolution_convert_fusion
  227.2 2.5 fusion.155
  229.7 2.5 fusion.156
  232.2 2.5 fusion.105
  234.7 37.0 %all-reduce.20.cloned.1.call-done = f32[512,1024]{1,0:T(8,128)} async-done(((f32[512,1024]{1,0:T(8,128)}), f32[512,1024]{1,0:T(8,128)}) %all-reduce.20.cloned.1.call-update) | async-done | bytes 2097168 | tf_op jit(solution)/shard_map/psum | solution.py:182
  271.7 3.5 multiply_reduce_fusion.1
  276.6 1.9 multiply_reduce_fusion.8
  281.6 20.4 %while.72 = (s32[]{:T(128)}, f32[1,128,256]{2,1,0:T(8,128)}, bf16[1,128,256]{2,1,0:T(8,128)(2,1)S(1)}, f32[1,128]{1,0:T(1,128)S(1)}, f32[1,128,256]{2,1,0:T(8,128)S(1)}, /*index=5*/s32[]{:T(128)}) while((s32[]{:T(128)}, f32[1,128,256]{2,1,0:T(8,128)}, bf16[1,128,256]{2,1,0:T(8,128)(2,1)S(1)}, f32[1,128]{1,0:T(1,128)S(1)}, ...), condition=%wide.region_16.17_spmd, body=%wide.region_15.16_spmd.sunk | while | flops 131074 | bytes 655981 | solution.py:199
  282.8 4.9 collective-permute-done.1
  289.7 4.9 collective-permute-done.1
  296.5 4.9 collective-permute-done.1
  306.0 99.6 %while.74 = (s32[]{:T(128)}, f32[1,128,256]{1,2,0:T(8,128)S(1)}, f32[8,1,64,128]{3,2,1,0:T(8,128)}, f32[8,1,64,128]{3,2,1,0:T(8,128)}, f32[8,1,64,256]{3,2,1,0:T...) while((s32[]{:T(128)}, f32[1,128,256]{1,2,0:T(8,128)S(1)}, ...), condition=%wide.region_27.28_spmd, body=%wide.region_20.27_spmd.sunk | while | flops 139747328 | bytes 3924165 | solution.py:55
  314.4 2.2 fusion.272
  326.8 2.2 fusion.272
  339.3 2.2 fusion.272
  351.7 2.2 fusion.272
  364.2 2.2 fusion.272
  376.6 2.2 fusion.272
  389.1 2.2 fusion.272
  401.5 2.2 fusion.272
  405.6 2.2 copy.107
  413.0 3.0 multiply_reduce_fusion.7
  419.3 6.7 collective-permute-done.3
  432.5 17.3 %all-reduce.11 = (bf16[512,16]{0,1:T(8,128)(2,1)}, bf16[256]{0:T(256)(128)(2,1)}) all-reduce(bf16[512,16]{0,1:T(8,128)(2,1)S(1)} %convolution_convert_fusion.4, bf16[256]{0:T(256)(128)(2,1)} %get-tuple-element.506), channel_id=1, replica_groups=mesh['dp'=2,'seq'=4,'tensor'=4] {'tensor'}, use_global_device_ids=true, to_apply=%region_29.30 | all-reduce | flops 8448 | bytes 33792 | tf_op jit(solution)/shard_map/psum | solution.py:243
  451.6 2.3 fusion.103
  460.4 38.9 %all-reduce.24.cloned.1.call-done = (bf16[512,1024]{1,0:T(8,128)(2,1)}, bf16[512,1024]{1,0:T(8,128)(2,1)}) async-done(((bf16[512,1024]{1,0:T(8,128)(2,1)}, bf16[512,1024]{1,0:T(8,128)(2,1)}), (bf16[512,1024]{1,0:T(8,128)(2,1)}, bf16[512,1024]{1,0:T(8,128)(2,1)})) %all-reduce.24.cloned.1.call-update) | async-done | bytes 2097168 | tf_op jit(solution)/shard_map/psum | solution.py:167
  499.4 3.6 fusion.87
  503.0 30.6 %all-reduce.9 = (f32[1024]{0:T(1024)}, f32[4,128]{1,0:T(4,128)}, f32[4,128]{1,0:T(4,128)}, f32[4,256]{1,0:T(4,128)}, f32[16,128]{1,0:T(8,128)}, /*index=5*/f32[128]{0:T(128)}, f32[256]{0:T(256)}, f32[1024]{0:T(1024)}) all-reduce(f32[1024]{0:T(1024)S(1)} %get-tuple-element.500, ...), channel_id=1, replica_groups=mesh['dp'=2,'seq'=4,'tensor'=4] {'dp','seq'}, use_global_device_ids=true, to_apply=%region_32.33 | all-reduce | flops 6528 | bytes 51712 | tf_op jit(solution)/shard_map/psum | solution.py:272
  533.7 2.7 fusion.101
  536.4 1.9 fusion.94
  538.2 230.7 %all-reduce.22.cloned.1.call-done = (f32[1024,128]{1,0:T(8,128)}, f32[1024,128]{1,0:T(8,128)}, f32[1024,256]{1,0:T(8,128)}, f32[1024,16]{0,1:T(8,128)}, f32[1024...) async-done(((f32[1024,128]{1,0:T(8,128)}, f32[1024,128]{1,0:T(8,128)}, f32[1024,256]{1,0:T(8,128)}, ...) | async-done | bytes 12910608 | tf_op jit(solution)/shard_map/psum | solution.py:272
  768.9 2.0 copy.220
  (609 shorter events, 243.0 us)
Async XLA Ops:
  7.2 189.5 %copy-start = (bf16[704,1024]{1,0:T(8,128)(2,1)S(1)}, bf16[704,1024]{1,0:T(8,128)(2,1)}, u32[]{:S(2)}) copy-start(bf16[704,1024]{1,0:T(8,128)(2,1)} %param.47) | copy-start | bytes 4325380
  7.2 4.6 copy-start.33
  7.2 182.7 %all-reduce.18.cloned.1.call-start = ((), (), s32[]{:S(2)}) async-start(), calls=%async_computation | async-start | bytes 4194304 | tf_op jit(solution)/shard_map/psum | solution.py:158
  8.1 4.2 copy-start.55
  12.3 6.8 copy-start.57
  12.8 6.7 copy-start.78
  12.8 6.7 copy-start.88
  13.3 9.1 %copy-start.79 = (bf16[4,256]{1,0:T(4,128)(2,1)S(1)}, bf16[4,256]{1,0:T(4,128)(2,1)}, u32[]{:S(2)}) copy-start(bf16[4,256]{1,0:T(4,128)(2,1)} %param.37) | copy-start | bytes 6148
  13.4 9.1 %copy-start.83 = (bf16[4,128]{1,0:T(4,128)(2,1)S(1)}, bf16[4,128]{1,0:T(4,128)(2,1)}, u32[]{:S(2)}) copy-start(bf16[4,128]{1,0:T(4,128)(2,1)} %param.36) | copy-start | bytes 3076
  13.4 9.0 %copy-start.84 = (bf16[4,128]{1,0:T(4,128)(2,1)S(1)}, bf16[4,128]{1,0:T(4,128)(2,1)}, u32[]{:S(2)}) copy-start(bf16[4,128]{1,0:T(4,128)(2,1)} %param.35) | copy-start | bytes 3076
  13.5 16.5 %collective-permute-start.2 = (bf16[1,3,512]{1,2,0:T(8,128)(2,1)S(1)}, bf16[1,3,512]{1,2,0:T(8,128)(2,1)}, u32[]{:S(2)}, u32[]{:S(2)}) collective-permute-start(bf16[1,3,512]{1,2,0:T(8,128)(2,1)S(1)} %slice.120), channel_id=1, source_target_pairs={{0,4},{4,8},{8,12},{1,5},{5,9},{9,13},{2,6},{6,10},{10,14},{3,7},{... | collective-permute-start | bytes 9224 | tf_op jit(solution)/shard_map/ppermute | solution.py:17
  19.5 4.6 copy-start.52
  23.0 8.2 %copy-start.59 = (f32[1,512]{1,0:T(1,128)}, f32[1,512]{1,0:T(1,128)S(1)}, u32[]{:S(2)}) copy-start(f32[1,512]{1,0:T(1,128)S(1)} %get-tuple-element.633) | copy-start | bytes 6148
  90.1 23.8 %copy-start.22 = (f32[8,1,64,128]{3,2,1,0:T(8,128)}, f32[8,1,64,128]{3,2,1,0:T(8,128)S(1)}, u32[]{:S(2)}) copy-start(f32[8,1,64,128]{3,2,1,0:T(8,128)S(1)} %get-tuple-element.1090) | copy-start | bytes 786436
  90.1 23.8 %copy-start.81 = (f32[256]{0:T(256)S(1)}, f32[256]{0:T(256)}, u32[]{:S(2)}) copy-start(f32[256]{0:T(256)} %convert_element_type.115) | copy-start | bytes 3076
  91.0 5.3 collective-permute-start
  97.0 6.8 collective-permute-start
  104.5 6.8 collective-permute-start
  117.2 72.7 %copy-start.12 = (bf16[1,512,1024]{2,1,0:T(8,128)(2,1)S(1)}, bf16[1,512,1024]{2,1,0:T(8,128)(2,1)}, u32[]{:S(2)}) copy-start(bf16[1,512,1024]{2,1,0:T(8,128)(2,1)} %param.29) | copy-start | bytes 3145732
  119.0 152.8 %all-reduce.20.cloned.1.call-start = ((), (), s32[]{:S(2)}) async-start(), calls=%async_computation.1 | async-start | bytes 4194304 | tf_op jit(solution)/shard_map/psum | solution.py:182
  201.9 297.4 %all-reduce.24.cloned.1.call-start = ((), (), s32[]{:S(2)}) async-start(), calls=%async_computation.3 | async-start | bytes 4194304 | tf_op jit(solution)/shard_map/psum | solution.py:167
  234.7 40.6 %copy-start.69 = (f32[512]{0:T(512)S(1)}, f32[512]{0:T(512)}, u32[]{:S(2)}) copy-start(f32[512]{0:T(512)} %copy-done.68) | copy-start | bytes 6148
  271.7 3.5 copy-start.5
  271.7 3.5 copy-start.16
  281.6 6.1 collective-permute-start.1
  288.4 6.1 collective-permute-start.1
  295.2 6.1 collective-permute-start.1
  405.6 7.4 copy-start.3
  405.6 7.4 copy-start.19
  417.7 8.3 %collective-permute-start.3 = (f32[1,3,512]{1,2,0:T(8,128)S(1)}, f32[1,3,512]{1,2,0:T(8,128)S(1)}, u32[]{:S(2)}, u32[]{:S(2)}) collective-permute-start(f32[1,3,512]{1,2,0:T(8,128)S(1)} %pad_add_fusion.1), channel_id=1, source_target_pairs={{4,0},{8,4},{12,8},{5,1},{9,5},{13,9},{6,2},{10,6},{14,10},{7,3},{... | collective-permute-start | bytes 18440 | tf_op jit(solution)/shard_map/ppermute | solution.py:17
  419.3 7.0 copy-start.34
  429.8 21.8 %copy-start.13 = (bf16[1,512,1024]{2,1,0:T(8,128)(2,1)S(1)}, bf16[1,512,1024]{2,1,0:T(8,128)(2,1)}, u32[]{:S(2)}) copy-start(bf16[1,512,1024]{2,1,0:T(8,128)(2,1)} %param.29) | copy-start | bytes 3145732
  429.8 339.1 %all-reduce.22.cloned.1.call-start = ((), (), s32[]{:S(2)}) async-start(), calls=%async_computation.2 | async-start | bytes 25821184 | tf_op jit(solution)/shard_map/psum | solution.py:272
  449.8 4.0 copy-start.10
  449.8 4.0 copy-start.46
  459.4 40.0 %copy-start.56 = (f32[1024]{0:T(1024)S(1)}, f32[1024]{0:T(1024)}, u32[]{:S(2)}) copy-start(f32[1024]{0:T(1024)} %copy-done.55) | copy-start | bytes 12292
  459.4 39.9 %copy-start.58 = (bf16[1024,16]{0,1:T(8,128)(2,1)S(1)}, bf16[1024,16]{0,1:T(8,128)(2,1)}, u32[]{:S(2)}) copy-start(bf16[1024,16]{0,1:T(8,128)(2,1)} %param.38) | copy-start | bytes 98308
  459.4 39.9 %copy-start.63 = (f32[512]{0:T(512)S(1)}, f32[512]{0:T(512)}, u32[]{:S(2)}) copy-start(f32[512]{0:T(512)} %copy-done.62) | copy-start | bytes 6148
  459.4 39.9 %copy-start.74 = (bf16[512,16]{0,1:T(8,128)(2,1)S(1)}, bf16[512,16]{0,1:T(8,128)(2,1)}, u32[]{:S(2)}) copy-start(bf16[512,16]{0,1:T(8,128)(2,1)} %get-tuple-element.595) | copy-start | bytes 49156
  499.3 3.7 copy-start.75
  499.3 3.7 copy-start.80
  499.4 3.6 copy-start.85
  499.4 34.3 %copy-start.65 = (f32[512]{0:T(512)S(1)}, f32[512]{0:T(512)}, u32[]{:S(2)}) copy-start(f32[512]{0:T(512)} %copy-done.64) | copy-start | bytes 6148
  499.4 34.3 %copy-start.6 = (f32[512,1024]{1,0:T(8,128)S(1)}, f32[512,1024]{1,0:T(8,128)}, u32[]{:S(2)}) copy-start(f32[512,1024]{1,0:T(8,128)} %copy-done.4) | copy-start | bytes 6291460
  768.9 3.9 copy-start.40
  768.9 4.9 copy-start.54
  768.9 5.5 copy-start.39
  779.9 4.4 copy-start.1
  (55 other events, 89.7 us)
Sparse Core Ops, SparseCore 0:
  119.1 70.7 all-reduce.17
  202.0 69.6 all-reduce.19
  430.0 69.3 all-reduce.23
  504.4 264.5 all-reduce.21
where the time goes:
time: 797 us; the launch traced here: 791 us
  waiting for transfers between devices  405 us (51%)
  local copies, waits for them, and re-layouts  105 us (13%)
  other arithmetic  97.9 us (12%)
  matrix products  96.3 us (12%)
  blocking collectives  47.9 us (6%)
  starting transfers between devices  22.6 us (3%)
  between operations  14.7 us (2%)
    psum x1, waiting for transfers between devices, on_device(): lax.psum((grad_attention_gain, grad_query_proj, grad_key_proj, grad_value...  231 us
    psum x1, waiting for transfers between devices, on_device(): middle_own = inputs_flat + lax.psum(mixer_part, 'tensor')  70 us
    psum x1, waiting for transfers between devices, on_device(): lax.psum(feed_part.astype(jnp.bfloat16), 'tensor').astype(jnp.float32)  38.9 us
    psum x1, waiting for transfers between devices, on_device(): two_grad_own = lax.psum(hidden_two_part, 'tensor')  37 us
    dot_general x24, other arithmetic, block_step(): jnp.einsum('ntd,nsd,ntsd->nts', queries, keylist, weights, precision=high...  36.2 us
    squeeze x40, local copies, waits for them, and re-layouts, recurrence(): lax.scan(jax.checkpoint(block_step), memory, (split_blocks(queries), spli...  31.4 us
    psum x1, blocking collectives, on_device(): lax.psum((grad_attention_gain, grad_query_proj, grad_key_proj, grad_value...  30.6 us
    ppermute x8, waiting for transfers between devices, shifted(): return lax.ppermute(x, axis, pairs)  28.7 us
  transfers between devices with their start and end apart: 12, of which 11 were waited for; matrix products, arithmetic and copies ran while one was open for 8% of the time, Pallas kernels for 0%

commit v1 on v0

--- a/solution.py
+++ b/solution.py
@@ -1,10 +1,13 @@
 import jax
 import jax.numpy as jnp
+import numpy as np
 from jax import lax
+from jax.experimental import pallas as pl
+from jax.experimental.pallas import tpu as pltpu
 from jax.sharding import PartitionSpec as P
 
 HEAD_KEY = 128
-SPAN = 64
+CHUNK = 128
 
 
 highest = lax.Precision.HIGHEST
@@ -30,34 +33,166 @@
     return jax.nn.silu(total)
 
 
-def block_step(memory, block):
-    queries, keylist, values, decays = block
-    extent = queries.shape[1]
-    cumul = jnp.cumsum(decays, axis=1)
-    causal = (jnp.arange(extent)[:, None] >= jnp.arange(extent)[None, :])[None, :, :, None]
-    spread = cumul[:, :, None, :] - cumul[:, None, :, :]
-    weights = jnp.where(causal, jnp.exp(jnp.where(causal, spread, 0.0)), 0.0)
-    scores = jnp.einsum("ntd,nsd,ntsd->nts", queries, keylist, weights, precision=highest)
-    inner = jnp.einsum("nts,nse->nte", scores, values, precision=highest)
-    carried = jnp.einsum("ntd,nde->nte", queries * jnp.exp(cumul), memory, precision=highest)
-    ending = cumul[:, -1:, :]
-    fresh = jnp.einsum("nsd,nse->nde", keylist * jnp.exp(ending - cumul), values, precision=highest)
-    return (jnp.exp(ending[:, 0, :])[:, :, None] * memory + fresh, inner + carried)
-
-
-def recurrence(queries, keylist, values, decays, memory):
-    groups, length, _ = queries.shape
-    blocks = length // SPAN
-
-    def split_blocks(array):
-        return jnp.moveaxis(array.reshape(groups, blocks, SPAN, array.shape[-1]), 1, 0)
-
-    memory, outputs = lax.scan(
-        jax.checkpoint(block_step),
-        memory,
-        (split_blocks(queries), split_blocks(keylist), split_blocks(values), split_blocks(decays)),
-    )
-    return (jnp.moveaxis(outputs, 0, 1).reshape(groups, length, -1), memory)
+def level_rows(chunk):
+    index = np.arange(chunk)
+    t, u = index[:, None], index[None, :]
+    parts = []
+    for level in range(chunk.bit_length() - 1):
+        half = 1 << level
+        last = (t // (2 * half)) * 2 * half + half - 1
+        upper = (t > last) & (u > last) & (u <= t)
+        lower = (t <= last) & (u > t) & (u <= last)
+        parts.append(upper | lower)
+    parts.append(u <= t)
+    parts.append(u > t)
+    return np.concatenate(parts, 0).astype(np.float32)
+
+
+def dot(a, b, ca=1, cb=0):
+    return lax.dot_general(
+        a.astype(jnp.bfloat16),
+        b.astype(jnp.bfloat16),
+        (((ca,), (cb,)), ((), ())),
+        preferred_element_type=jnp.float32,
+    )
+
+
+def chunk_factors(rows, decays):
+    top = decays.astype(jnp.bfloat16)
+    rest = (decays - top.astype(jnp.float32)).astype(jnp.bfloat16)
+    both = dot(rows, jnp.concatenate([top, rest], 1))
+    return both[:, :HEAD_KEY] + both[:, HEAD_KEY:]
+
+
+def grids(chunk):
+    t = lax.broadcasted_iota(jnp.int32, (chunk, chunk), 0)
+    s = lax.broadcasted_iota(jnp.int32, (chunk, chunk), 1)
+    r = lax.broadcasted_iota(jnp.int32, (chunk, HEAD_KEY), 0)
+    return t, s, r
+
+
+def chunk_scores(queries, keylist, factors, t, s, r, levels):
+    chunk = queries.shape[0]
+    mixed = t ^ s
+    scores = jnp.where(
+        t == s, jnp.sum(queries * keylist, axis=1, keepdims=True), 0.0
+    )
+    sides = []
+    for level in range(levels):
+        factor = factors[level * chunk : (level + 1) * chunk]
+        side = (jnp.where(((r >> level) & 1) == 1, queries, keylist) * factor).astype(jnp.bfloat16)
+        sides.append(side)
+        product = dot(side, side, 1, 1)
+        scores = jnp.where(((mixed >> level) == 1) & (t > s), product, scores)
+    return scores, sides
+
+
+def forward_kernel(rows_ref, q_ref, k_ref, v_ref, g_ref, o_ref, dq_ref, st_ref, off_ref, last_ref):
+    chunk = rows_ref.shape[1]
+    count = q_ref.shape[1] // chunk
+    levels = chunk.bit_length() - 1
+    rows = rows_ref[...]
+    t, s, r = grids(chunk)
+    state = jnp.zeros((v_ref.shape[2], HEAD_KEY), jnp.float32)
+    offset = jnp.zeros((1, HEAD_KEY), jnp.float32)
+    for c in range(count):
+        part = pl.ds(c * chunk, chunk)
+        queries, keylist, values = q_ref[0, part], k_ref[0, part], v_ref[0, part]
+        raw = chunk_factors(rows, g_ref[0, part])
+        factors = jnp.exp(raw)
+        pre = factors[levels * chunk : (levels + 1) * chunk]
+        suf = factors[(levels + 1) * chunk :]
+        scores, _ = chunk_scores(queries, keylist, factors, t, s, r, levels)
+        st_ref[0, c] = state
+        off_ref[0, c] = jnp.broadcast_to(offset, (8, HEAD_KEY))
+        queries_pre = queries * pre
+        o_ref[0, part] = dot(scores, values) + dot(queries_pre, state, 1, 1)
+        dq_ref[0, part] = queries_pre * jnp.exp(offset)
+        state = state * pre[chunk - 1 :] + dot(values, keylist * suf, 0, 0)
+        offset = offset + raw[(levels + 1) * chunk - 1 : (levels + 1) * chunk]
+    off_ref[0, count] = jnp.broadcast_to(offset, (8, HEAD_KEY))
+    last_ref[0] = state
+
+
+def backward_kernel(
+    rows_ref, rowst_ref, q_ref, k_ref, v_ref, g_ref, do_ref, st_ref, off_ref, inc_ref, out_ref,
+    dq_ref, dk_ref, dv_ref, dg_ref,
+):
+    chunk = rows_ref.shape[1]
+    count = q_ref.shape[1] // chunk
+    levels = chunk.bit_length() - 1
+    rows = rows_ref[...]
+    rowst = rowst_ref[...]
+    t, s, r = grids(chunk)
+    mixed = t ^ s
+    pull = out_ref[0]
+    incoming = inc_ref[0]
+    for c in reversed(range(count)):
+        part = pl.ds(c * chunk, chunk)
+        queries, keylist, values = q_ref[0, part], k_ref[0, part], v_ref[0, part]
+        outer = do_ref[0, part]
+        factors = jnp.exp(chunk_factors(rows, g_ref[0, part]))
+        pre = factors[levels * chunk : (levels + 1) * chunk]
+        suf = factors[(levels + 1) * chunk :]
+        scores, sides = chunk_scores(queries, keylist, factors, t, s, r, levels)
+        state = st_ref[0, c] + incoming * jnp.exp(off_ref[0, c][:1])
+        lower = dot(outer, values, 1, 1)
+        upper = dot(values, outer, 1, 1)
+        both = jnp.where(t > s, lower, upper)
+        own = jnp.sum(outer * values, axis=1, keepdims=True)
+        dq = own * keylist
+        dk = own * queries
+        shares = []
+        for level in range(levels):
+            factor = factors[level * chunk : (level + 1) * chunk]
+            back = dot(jnp.where((mixed >> level) == 1, both, 0.0), sides[level]) * factor
+            bit = ((r >> level) & 1) == 1
+            dq = dq + jnp.where(bit, back, 0.0)
+            dk = dk + jnp.where(bit, 0.0, back)
+            shares.append((back * jnp.where(bit, queries, keylist)).astype(jnp.bfloat16))
+        from_state = dot(outer, state) * pre
+        to_state = dot(values, pull) * suf
+        dq = dq + from_state
+        dk = dk + to_state
+        shares.append((from_state * queries).astype(jnp.bfloat16))
+        shares.append((to_state * keylist).astype(jnp.bfloat16))
+        ending = pre[chunk - 1 :]
+        whole = jnp.sum(state * pull, axis=0, keepdims=True) * ending
+        dg = dot(rowst, jnp.concatenate(shares, 0)) + whole
+        dq_ref[0, part] = dq
+        dk_ref[0, part] = dk
+        dg_ref[0, part] = dg
+        dv_ref[0, part] = dot(scores, outer, 0, 0) + dot(keylist * suf, pull, 1, 1)
+        pull = pull * ending + dot(outer, queries * pre, 0, 0)
+
+
+def group_spec(shape):
+    extra = len(shape) - 1
+    return pl.BlockSpec((1,) + tuple(shape[1:]), lambda i: (i,) + (0,) * extra)
+
+
+def whole_spec(shape):
+    return pl.BlockSpec(tuple(shape), lambda i: (0,) * len(shape))
+
+
+def run_groups(kernel, constants, arrays, outs, flops):
+    return pl.pallas_call(
+        kernel,
+        grid=(arrays[0].shape[0],),
+        in_specs=[whole_spec(a.shape) for a in constants] + [group_spec(a.shape) for a in arrays],
+        out_specs=[group_spec(o) for o in outs],
+        out_shape=[jax.ShapeDtypeStruct(o, jnp.float32) for o in outs],
+        compiler_params=pltpu.CompilerParams(vmem_limit_bytes=48 * 1024 * 1024),
+        cost_estimate=pl.CostEstimate(flops=flops, bytes_accessed=4000000, transcendentals=0),
+    )(*constants, *arrays)
+
+
+def state_chain(states, totals, order, me):
+    carried = jnp.zeros_like(states[0])
+    for j in order:
+        follow = (j < me) if order[0] == 0 else (j > me)
+        carried = jnp.where(follow, jnp.exp(totals[j]) * carried + states[j], carried)
+    return carried
 
 
 def to_heads(array, width):
@@ -84,6 +219,11 @@
 
 def feed_piece(gate_pre, lift_pre):
     return jax.nn.silu(gate_pre) * lift_pre
+
+
+def split_sum(grads):
+    sums = lax.psum(tuple(g.astype(jnp.bfloat16) for g in grads), ("dp", "seq"))
+    return tuple(g.astype(jnp.float32) for g in sums)
 
 
 def on_device(
@@ -134,20 +274,39 @@
     decay_logit = jnp.dot(low_rank, decay_up.astype(jnp.float32), precision=highest) + decay_bias
     log_decay = jax.nn.log_sigmoid(decay_logit) / 16.0
     decays = to_heads(log_decay.reshape(batch, seglen, key_width), HEAD_KEY)
-    zero_state = jnp.zeros((queries.shape[0], HEAD_KEY, head_value), jnp.float32)
-    local_out, local_state = recurrence(queries, keylist, values, decays, zero_state)
-    cumul = jnp.cumsum(decays, axis=1)
-    total = jnp.exp(cumul[:, -1])
-    decayed_q = queries * jnp.exp(cumul)
-
-    def forward_turn(turn, carry):
-        received = shifted(carry[1], "seq", 1)
-        return (received, total[:, :, None] * received + local_state)
-
-    incoming, _ = lax.fori_loop(
-        0, lax.axis_size("seq") - 1, forward_turn, (zero_state, local_state)
-    )
-    recurrent = local_out + jnp.einsum("ntd,nde->nte", decayed_q, incoming, precision=highest)
+    groups = queries.shape[0]
+    chunk = min(CHUNK, seglen)
+    count = seglen // chunk
+    row_table = level_rows(chunk)
+    rows_const = jnp.asarray(row_table, jnp.bfloat16)
+    rowst_const = jnp.asarray(row_table.T, jnp.bfloat16)
+    flops = groups * seglen * 3000000
+    local_out, decayed_q, states, offsets, local_state = run_groups(
+        forward_kernel,
+        (rows_const,),
+        (queries, keylist, values, decays),
+        (
+            (groups, seglen, head_value),
+            (groups, seglen, HEAD_KEY),
+            (groups, count, head_value, HEAD_KEY),
+            (groups, count + 1, 8, HEAD_KEY),
+            (groups, head_value, HEAD_KEY),
+        ),
+        flops,
+    )
+    seq_size = lax.axis_size("seq")
+    seq_me = lax.axis_index("seq")
+    gathered = lax.all_gather(
+        jnp.concatenate([local_state, offsets[:, count]], 1), "seq"
+    )
+    totals = gathered[:, :, head_value : head_value + 1]
+    incoming = state_chain(
+        gathered[:, :, :head_value], totals, list(range(seq_size)), seq_me
+    )
+    recurrent = local_out + jnp.einsum(
+        "ntd,ned->nte", decayed_q.astype(jnp.bfloat16), incoming.astype(jnp.bfloat16),
+        preferred_element_type=jnp.float32,
+    )
     recurrent = from_heads(recurrent, batch).reshape(batch, seglen, -1, head_value)
     swish_gate = jnp.dot(hidden, swish_proj, preferred_element_type=jnp.float32).reshape(
         batch, seglen, -1, head_value
@@ -155,7 +314,7 @@
     gated_f, head_back = jax.vjp(head_piece, recurrent, swish_gate, head_gain.astype(jnp.float32))
     gated = gated_f.astype(jnp.bfloat16).reshape(rows, value_width)
     mixer_part = jnp.dot(gated, output_proj, preferred_element_type=jnp.float32)
-    middle_own = inputs_flat + lax.psum(mixer_part, "tensor")
+    middle_own = inputs_flat + lax.psum(mixer_part.astype(jnp.bfloat16), "tensor").astype(jnp.float32)
     hidden_two_own, norm_two_back = jax.vjp(root_norm, middle_own, feed_gain_f)
     hidden_two = hidden_two_own.astype(jnp.bfloat16)
     gate_pre = jnp.dot(hidden_two, feed_gate, preferred_element_type=jnp.float32)
@@ -179,7 +338,7 @@
     hidden_two_part = jnp.dot(
         gate_pre_grad, feed_gate.T, preferred_element_type=jnp.float32
     ) + jnp.dot(lift_pre_grad, feed_lift.T, preferred_element_type=jnp.float32)
-    two_grad_own = lax.psum(hidden_two_part, "tensor")
+    two_grad_own = lax.psum(hidden_two_part.astype(jnp.bfloat16), "tensor").astype(jnp.float32)
     middle_norm_grad, grad_feed_gain = norm_two_back(two_grad_own)
     middle_grad_own = upstream + middle_norm_grad
     mixer_grad = middle_grad_own.astype(jnp.bfloat16)
@@ -190,18 +349,28 @@
     recurrent_grad, swish_grad, head_gain_part = head_back(gated_grad)
     swish_gate_grad = swish_grad.reshape(rows, value_width).astype(jnp.bfloat16)
     recurrent_grad = to_heads(recurrent_grad.reshape(batch, seglen, value_width), head_value)
-    local_pull = jnp.einsum("ntd,nte->nde", decayed_q, recurrent_grad, precision=highest)
-
-    def backward_turn(turn, carry):
-        received = shifted(carry[1].astype(jnp.bfloat16), "seq", -1).astype(jnp.float32)
-        return (received, total[:, :, None] * received + local_pull)
-
-    outgoing_grad, _ = lax.fori_loop(
-        0, lax.axis_size("seq") - 1, backward_turn, (zero_state, local_pull)
-    )
-    _, recurrence_back = jax.vjp(recurrence, queries, keylist, values, decays, incoming)
-    queries_grad, keys_grad, values_grad, decays_grad, _ = recurrence_back(
-        (recurrent_grad, outgoing_grad)
+    local_pull = jnp.einsum(
+        "ntd,nte->ned", decayed_q.astype(jnp.bfloat16), recurrent_grad.astype(jnp.bfloat16),
+        preferred_element_type=jnp.float32,
+    )
+    pulls = lax.all_gather(local_pull.astype(jnp.bfloat16), "seq").astype(jnp.float32)
+    outgoing_grad = state_chain(pulls, totals, list(range(seq_size))[::-1], seq_me)
+    queries_grad, keys_grad, values_grad, decays_grad = run_groups(
+        backward_kernel,
+        (rows_const, rowst_const),
+        (
+            queries,
+            keylist,
+            values,
+            decays,
+            recurrent_grad,
+            states,
+            offsets,
+            incoming,
+            outgoing_grad,
+        ),
+        (queries.shape, queries.shape, values.shape, queries.shape),
+        2 * flops,
     )
     activated_grad = jnp.concatenate(
         [
@@ -251,46 +420,39 @@
     grad_query_conv = conv_grad[:, :key_width]
     grad_key_conv = conv_grad[:, key_width : 2 * key_width]
     grad_value_conv = conv_grad[:, 2 * key_width :]
-    (
+    grad_query_proj, grad_key_proj, grad_value_proj, grad_swish_proj = split_sum(
+        (grad_query_proj, grad_key_proj, grad_value_proj, grad_swish_proj)
+    )
+    (grad_output_proj,) = split_sum((grad_output_proj,))
+    grad_feed_gate, grad_feed_lift = split_sum((grad_feed_gate, grad_feed_lift))
+    (grad_feed_down,) = split_sum((grad_feed_down,))
+    small = (
         grad_attention_gain,
-        grad_query_proj,
-        grad_key_proj,
-        grad_value_proj,
         grad_query_conv,
         grad_key_conv,
         grad_value_conv,
         grad_decay_down,
         grad_decay_up,
         grad_decay_bias,
-        grad_swish_proj,
         grad_head_gain,
-        grad_output_proj,
         grad_feed_gain,
-        grad_feed_gate,
-        grad_feed_lift,
-        grad_feed_down,
-    ) = lax.psum(
-        (
-            grad_attention_gain,
-            grad_query_proj,
-            grad_key_proj,
-            grad_value_proj,
-            grad_query_conv,
-            grad_key_conv,
-            grad_value_conv,
-            grad_decay_down,
-            grad_decay_up,
-            grad_decay_bias,
-            grad_swish_proj,
-            grad_head_gain,
-            grad_output_proj,
-            grad_feed_gain,
-            grad_feed_gate,
-            grad_feed_lift,
-            grad_feed_down,
-        ),
-        ("dp", "seq"),
-    )
+    )
+    flat = lax.psum(jnp.concatenate([x.reshape(-1) for x in small]), ("dp", "seq"))
+    summed, start = [], 0
+    for x in small:
+        summed.append(flat[start : start + x.size].reshape(x.shape))
+        start += x.size
+    (
+        grad_attention_gain,
+        grad_query_conv,
+        grad_key_conv,
+        grad_value_conv,
+        grad_decay_down,
+        grad_decay_up,
+        grad_decay_bias,
+        grad_head_gain,
+        grad_feed_gain,
+    ) = summed
     return (
         mixed,
         tokens_grad,

time: 797 us -> 495 us (0.62)
  local copies, waits for them, and re-layouts: 105 us -> 19.7 us
  waiting for transfers between devices: 405 us -> 322 us
  other arithmetic: 97.9 us -> 36 us
  matrix products: 96.3 us -> 42.2 us
  starting transfers between devices: 22.6 us -> 6.61 us
    psum x3 -> x4, waiting for transfers between devices: 338 us -> 280 us  [the longest x1 138 us: split_sum(): lax.psum(tuple((g.astype(jnp.bfloat16) for g in grads)), ('dp', 'seq'))]
    dot_general x82 -> x2, matrix products: 53.9 us -> 0.85 us  [the longest x1 0.48 us: on_device(): jnp.einsum('ntd,nte->ned', decayed_q.astype(jnp.bfloat16), recurrent_grad...]
    dot_general x24 -> x0, other arithmetic: 36.2 us -> none  [block_step(): jnp.einsum('ntd,nsd,ntsd->nts', queries, keylist, weights, precision=high...]
    squeeze x64 -> x1, local copies, waits for them, and re-layouts: 31.5 us -> 0.01 us  [on_device(): offsets[:, count]]
    psum x1 -> x0, blocking collectives: 30.6 us -> none  [on_device(): lax.psum((grad_attention_gain, grad_query_proj, grad_key_proj, grad_value...]
    all_gather x0 -> x2, blocking collectives: none -> 30.2 us  [the longest x1 16.1 us: on_device(): lax.all_gather(jnp.concatenate([local_state, offsets[:, count]], 1), 'seq')]
    ppermute x8 -> x2, waiting for transfers between devices: 28.7 us -> 4.22 us  [shifted(): return lax.ppermute(x, axis, pairs)]
    reduce_sum x24 -> x0, other arithmetic: 18 us -> none  [the longest x8 17.3 us: block_step(): spread = cumul[:, :, None, :] - cumul[:, None, :, :]]
  transfers between devices with their start and end apart: 12 -> 7, of which waited for: 11 -> 7; matrix products, arithmetic and copies ran while one was open for 8% -> 8% of each run, Pallas kernels for 0% -> 0%
where the time goes in v1:
time: 495 us; the launch traced here: 494 us
  waiting for transfers between devices  322 us (65%)
  blocking collectives  46.6 us (9%)
  matrix products  42.2 us (9%)
  other arithmetic  36 us (7%)
  local copies, waits for them, and re-layouts  19.7 us (4%)
  between operations  14.8 us (3%)
  starting transfers between devices  6.61 us (1%)
  Pallas kernels  6.33 us (1%)
    psum x1, waiting for transfers between devices, split_sum(): lax.psum(tuple((g.astype(jnp.bfloat16) for g in grads)), ('dp', 'seq'))  138 us
    psum x1, waiting for transfers between devices, on_device(): lax.psum(mixer_part.astype(jnp.bfloat16), 'tensor').astype(jnp.float32)  54 us
    psum x1, waiting for transfers between devices, on_device(): lax.psum(jnp.concatenate([x.reshape(-1) for x in small]), ('dp', 'seq'))  44.1 us
    psum x1, waiting for transfers between devices, on_device(): lax.psum(hidden_two_part.astype(jnp.bfloat16), 'tensor').astype(jnp.float32)  43.9 us
    psum x1, waiting for transfers between devices, on_device(): lax.psum(feed_part.astype(jnp.bfloat16), 'tensor').astype(jnp.float32)  37.6 us
    psum x1, blocking collectives, on_device(): lax.psum(low_rank_part.astype(jnp.bfloat16), 'tensor').astype(jnp.float32)  16.3 us
    all_gather x1, blocking collectives, on_device(): lax.all_gather(jnp.concatenate([local_state, offsets[:, count]], 1), 'seq')  16.1 us
    all_gather x1, blocking collectives, on_device(): lax.all_gather(local_pull.astype(jnp.bfloat16), 'seq').astype(jnp.float32)  14.2 us
  transfers between devices with their start and end apart: 7, of which 7 were waited for; matrix products, arithmetic and copies ran while one was open for 8% of the time, Pallas kernels for 0%

profile of v1, /device:TPU:0, one launch (start us, length us, event | category | flops | bytes accessed | tf_op | source)
XLA Modules:
  0.0 494.4 jit_solution(16867670974514993137)
XLA Ops:
  8.1 1.5 fusion.12
  9.6 1.9 convolution_convert_fusion.10
  12.7 4.9 collective-permute-start
  20.2 1.6 fusion.36
  22.8 2.2 shard_map.348
  25.1 16.1 %all-gather = f32[4,264,128]{2,1,0:T(8,128)S(1)} all-gather(f32[1,264,128]{2,1,0:T(8,128)S(1)} %pad_maximum_fusion.2), channel_id=2, replica_groups=mesh['dp'=2,'seq'=4,'tensor'=4] {'seq'}, dimensions={0}, use_global_device_ids=true | all-gather | bytes 675840 | tf_op jit(solution)/shard_map/all_gather | solution.py:299
  42.0 1.3 multiply_convert_fusion.3
  44.0 1.4 convolution_convert_fusion.4
  45.7 54.0 %all-reduce.17.cloned.1.call-done = bf16[512,1024]{1,0:T(8,128)(2,1)} async-done(((bf16[512,1024]{1,0:T(8,128)(2,1)}), bf16[512,1024]{1,0:T(8,128)(2,1)}) %all-reduce.17.cloned.1.call-update) | async-done | bytes 1048592 | tf_op jit(solution)/shard_map/psum | solution.py:317
  99.7 2.1 multiply_reduce_fusion
  106.1 2.3 multiply_convert_fusion.1
  109.5 2.0 add_convert_fusion.1
  112.8 3.6 convolution_convert_fusion.1
  116.4 2.0 convolution_convert_fusion
  118.4 2.0 convolution_convert_fusion.3
  120.4 43.9 %all-reduce.19.cloned.1.call-done = bf16[512,1024]{1,0:T(8,128)(2,1)} async-done(((bf16[512,1024]{1,0:T(8,128)(2,1)}), bf16[512,1024]{1,0:T(8,128)(2,1)}) %all-reduce.19.cloned.1.call-update) | async-done | bytes 1048592 | tf_op jit(solution)/shard_map/psum | solution.py:341
  164.2 3.5 fusion.16
  167.9 2.2 fusion.17
  172.1 14.2 %all-gather.1 = bf16[1024,128]{1,0:T(8,128)(2,1)S(1)} all-gather(bf16[256,128]{1,0:T(8,128)(2,1)S(1)} %convolution_convert_fusion.13), channel_id=3, replica_groups=mesh['dp'=2,'seq'=4,'tensor'=4] {'seq'}, dimensions={0}, use_global_device_ids=true | all-gather | bytes 327680 | tf_op jit(solution)/shard_map/all_gather | solution.py:356
  186.4 4.1 shard_map.349
  192.2 1.3 collective-permute-start.1
  193.7 4.1 collective-permute-done.1
  199.8 1.6 add_convert_fusion
  202.6 3.1 convolution_convert_fusion.2
  207.2 16.3 %all-reduce.9 = (bf16[512,16]{0,1:T(8,128)(2,1)S(1)}, bf16[256]{0:T(256)(128)(2,1)}) all-reduce(bf16[512,16]{0,1:T(8,128)(2,1)S(1)} %convolution_convert_fusion.14, bf16[256]{0:T(256)(128)(2,1)S(1)} %get-tuple-element.83), channel_id=1, replica_groups=mesh['dp'=2,'seq'=4,'tensor'=4] {'tensor'}, use_global_device_ids=true, to_apply=%region_9.10 | all-reduce | flops 8448 | bytes 33792 | tf_op jit(solution)/shard_map/psum | solution.py:412
  223.6 1.4 fusion.96
  225.0 1.4 reshape.790
  226.4 2.5 convolution_convert_fusion.6
  228.9 1.3 convolution_convert_fusion.5
  230.3 1.4 convolution_convert_fusion.9
  231.6 1.5 convolution_convert_fusion.7
  233.1 37.6 %all-reduce.25.cloned.1.call-done = (bf16[512,1024]{1,0:T(8,128)(2,1)}, bf16[512,1024]{1,0:T(8,128)(2,1)}) async-done(((bf16[512,1024]{1,0:T(8,128)(2,1)}, bf16[512,1024]{1,0:T(8,128)(2,1)}), (bf16[512,1024]{1,0:T(8,128)(2,1)}, bf16[512,1024]{1,0:T(8,128)(2,1)})) %all-reduce.25.cloned.1.call-update) | async-done | bytes 2097168 | tf_op jit(solution)/shard_map/psum | solution.py:326
  270.8 3.4 fusion.11
  275.3 1.4 convolution_convert_fusion.8
  278.2 4.7 fusion.19
  282.9 44.1 %all-reduce.21.cloned.1.call-done = f32[22912]{0:T(1024)} async-done(((f32[22912]{0:T(1024)}), f32[22912]{0:T(1024)}) %all-reduce.21.cloned.1.call-update) | async-done | bytes 91664 | tf_op jit(solution)/shard_map/psum | solution.py:440
  327.0 1.3 fusion.110
  330.8 1.2 slice.266
  331.9 1.2 slice.267
  333.2 1.3 slice_bitcast_fusion.6
  334.5 1.3 slice_bitcast_fusion.4
  335.8 138.2 %all-reduce.23.cloned.1.call-done = (bf16[1024,128]{1,0:T(8,128)(2,1)}, bf16[1024,128]{1,0:T(8,128)(2,1)}, bf16[1024,256]{1,0:T(8,128)(2,1)}, bf16[1024,256]{1,0...) async-done(((bf16[1024,128]{1,0:T(8,128)(2,1)}, bf16[1024,128]{1,0:T(8,128)(2,1)}, ...) | async-done | bytes 6422544 | tf_op jit(solution)/shard_map/psum | solution.py:225
  474.1 1.8 convert_element_type.225
  475.9 1.8 convert_element_type.227
  477.7 2.2 convert_element_type.229
  482.1 1.9 convert_element_type.237
  484.0 1.9 convert_element_type.239
  486.0 1.9 convert_element_type.241
  (235 shorter events, 29.4 us)
Async XLA Ops:
  7.2 98.7 %copy-start = (bf16[704,1024]{1,0:T(8,128)(2,1)S(1)}, bf16[704,1024]{1,0:T(8,128)(2,1)}, u32[]{:S(2)}) copy-start(bf16[704,1024]{1,0:T(8,128)(2,1)} %param.39) | copy-start | bytes 4325380
  7.2 4.3 copy-start.8
  7.2 4.3 copy-start.51
  7.2 92.5 %all-reduce.17.cloned.1.call-start = ((), (), s32[]{:S(2)}) async-start(), calls=%async_computation | async-start | bytes 2097152 | tf_op jit(solution)/shard_map/psum | solution.py:317
  9.6 214.0 %copy-start.60 = (f32[512]{0:T(512)}, f32[512]{0:T(512)S(1)}, u32[]{:S(2)}) copy-start(f32[512]{0:T(512)S(1)} %fusion.82) | copy-start | bytes 6148
  12.1 5.6 %copy-start.70 = (bf16[1024,16]{0,1:T(8,128)(2,1)S(1)}, bf16[1024,16]{0,1:T(8,128)(2,1)}, u32[]{:S(2)}) copy-start(bf16[1024,16]{0,1:T(8,128)(2,1)} %param.30) | copy-start | bytes 98308
  12.6 5.6 %copy-start.57 = (bf16[16,128]{1,0:T(8,128)(2,1)S(1)}, bf16[16,128]{1,0:T(8,128)(2,1)}, u32[]{:S(2)}) copy-start(bf16[16,128]{1,0:T(8,128)(2,1)} %param.31) | copy-start | bytes 12292
  12.6 5.5 %copy-start.66 = (f32[128]{0:T(128)S(1)}, f32[128]{0:T(128)}, u32[]{:S(2)}) copy-start(f32[128]{0:T(128)} %param.32) | copy-start | bytes 1540
  12.6 6.1 %copy-start.63 = (bf16[4,256]{1,0:T(4,128)(2,1)S(1)}, bf16[4,256]{1,0:T(4,128)(2,1)}, u32[]{:S(2)}) copy-start(bf16[4,256]{1,0:T(4,128)(2,1)} %param.29) | copy-start | bytes 6148
  12.6 6.1 %copy-start.64 = (bf16[4,128]{1,0:T(4,128)(2,1)S(1)}, bf16[4,128]{1,0:T(4,128)(2,1)}, u32[]{:S(2)}) copy-start(bf16[4,128]{1,0:T(4,128)(2,1)} %param.28) | copy-start | bytes 3076
  12.6 6.1 %copy-start.65 = (bf16[4,128]{1,0:T(4,128)(2,1)S(1)}, bf16[4,128]{1,0:T(4,128)(2,1)}, u32[]{:S(2)}) copy-start(bf16[4,128]{1,0:T(4,128)(2,1)} %param.27) | copy-start | bytes 3076
  12.6 6.2 %copy-start.72 = (bf16[256]{0:T(256)(128)(2,1)S(1)}, bf16[256]{0:T(256)(128)(2,1)}, u32[]{:S(2)}) copy-start(bf16[256]{0:T(256)(128)(2,1)} %param.34) | copy-start | bytes 1540
  12.7 6.1 %copy-start.29 = (bf16[1,512,512]{2,1,0:T(8,128)(2,1)}, bf16[1,512,512]{2,1,0:T(8,128)(2,1)S(1)}, u32[]{:S(2)}) copy-start(bf16[1,512,512]{2,1,0:T(8,128)(2,1)S(1)} %maximum_bitcast_fusion) | copy-start | bytes 1572868
  12.7 6.2 %collective-permute-start = (bf16[1,3,512]{2,1,0:T(4,128)(2,1)S(1)}, bf16[1,3,512]{2,1,0:T(4,128)(2,1)S(1)}, u32[]{:S(2)}, u32[]{:S(2)}) collective-permute-start(bf16[1,3,512]{2,1,0:T(4,128)(2,1)S(1)} %slice.236), channel_id=1, source_target_pairs={{0,4},{4,8},{8,12},{1,5},{5,9},{9,13},{2,6},{6,10},{10,14},{3,7},{... | collective-permute-start | bytes 9224 | tf_op jit(solution)/shard_map/ppermute | solution.py:20
  25.0 18.3 %copy-start.4 = (f32[1,4,256,128]{3,2,1,0:T(8,128)}, f32[1,4,256,128]{3,2,1,0:T(8,128)S(1)}, u32[]{:S(2)}) copy-start(f32[1,4,256,128]{3,2,1,0:T(8,128)S(1)} %get-tuple-element.32.st_ref) | copy-start | bytes 1572868
  25.0 16.9 %copy-start.9 = (bf16[1,512,1024]{2,1,0:T(8,128)(2,1)S(1)}, bf16[1,512,1024]{2,1,0:T(8,128)(2,1)}, u32[]{:S(2)}) copy-start(bf16[1,512,1024]{2,1,0:T(8,128)(2,1)} %param.21) | copy-start | bytes 3145732
  25.0 16.9 %copy-start.42 = (bf16[1024,256]{1,0:T(8,128)(2,1)S(1)}, bf16[1024,256]{1,0:T(8,128)(2,1)}, u32[]{:S(2)}) copy-start(bf16[1024,256]{1,0:T(8,128)(2,1)} %param.33) | copy-start | bytes 1572868
  45.4 118.8 %all-reduce.19.cloned.1.call-start = ((), (), s32[]{:S(2)}) async-start(), calls=%async_computation.1 | async-start | bytes 2097152 | tf_op jit(solution)/shard_map/psum | solution.py:341
  111.5 159.2 %all-reduce.25.cloned.1.call-start = ((), (), s32[]{:S(2)}) async-start(), calls=%async_computation.4 | async-start | bytes 4194304 | tf_op jit(solution)/shard_map/psum | solution.py:326
  112.7 3.6 copy-start.35
  112.8 3.6 copy-start.75
  120.4 47.5 %copy-start.11 = (bf16[1,512,1024]{2,1,0:T(8,128)(2,1)S(1)}, bf16[1,512,1024]{2,1,0:T(8,128)(2,1)}, u32[]{:S(2)}) copy-start(bf16[1,512,1024]{2,1,0:T(8,128)(2,1)} %param.21) | copy-start | bytes 3145732
  164.2 3.6 copy-start.14
  164.2 3.6 copy-start.22
  171.4 28.4 %copy-start.53 = (bf16[512,256]{1,0:T(8,128)(2,1)}, bf16[512,256]{1,0:T(8,128)(2,1)S(1)}, u32[]{:S(2)}) copy-start(bf16[512,256]{1,0:T(8,128)(2,1)S(1)} %get-tuple-element.106) | copy-start | bytes 786436
  171.4 15.0 %copy-start.3 = (bf16[128,1152]{1,0:T(8,128)(2,1)S(1)}, bf16[128,1152]{1,0:T(8,128)(2,1)}, u32[]{:S(2)}) copy-start(bf16[128,1152]{1,0:T(8,128)(2,1)} %constant.54.clone.rowst_ref) | copy-start | bytes 884740
  171.4 15.0 %copy-start.5 = (f32[1,4,256,128]{3,2,1,0:T(8,128)S(1)}, f32[1,4,256,128]{3,2,1,0:T(8,128)}, u32[]{:S(2)}) copy-start(f32[1,4,256,128]{3,2,1,0:T(8,128)} %copy-done.4) | copy-start | bytes 1572868
  186.4 4.1 copy-start.7
  186.4 4.1 copy-start.23
  192.2 5.5 %collective-permute-start.1 = (f32[1,3,512]{2,1,0:T(4,128)S(1)}, f32[1,3,512]{2,1,0:T(4,128)S(1)}, u32[]{:S(2)}, u32[]{:S(2)}) collective-permute-start(f32[1,3,512]{2,1,0:T(4,128)S(1)} %pad_add_fusion.1), channel_id=1, source_target_pairs={{4,0},{8,4},{12,8},{5,1},{9,5},{13,9},{6,2},{10,6},{14,10},{7,3},{... | collective-permute-start | bytes 18440 | tf_op jit(solution)/shard_map/ppermute | solution.py:20
  193.7 4.6 copy-start.20
  193.7 4.1 copy-start.48
  201.4 5.0 %copy-start.26 = (f32[512,128]{1,0:T(8,128)S(1)}, f32[512,128]{1,0:T(8,128)}, u32[]{:S(2)}) copy-start(f32[512,128]{1,0:T(8,128)} %copy-done.25) | copy-start | bytes 786436
  201.4 22.1 %copy-start.12 = (bf16[1,512,1024]{2,1,0:T(8,128)(2,1)S(1)}, bf16[1,512,1024]{2,1,0:T(8,128)(2,1)}, u32[]{:S(2)}) copy-start(bf16[1,512,1024]{2,1,0:T(8,128)(2,1)} %param.21) | copy-start | bytes 3145732
  201.5 125.5 %all-reduce.21.cloned.1.call-start = ((), (), s32[]{:S(2)}) async-start(), calls=%async_computation.2 | async-start | bytes 188416 | tf_op jit(solution)/shard_map/psum | solution.py:440
  207.0 16.6 %copy-start.27 = (f32[512,128]{1,0:T(8,128)}, f32[512,128]{1,0:T(8,128)S(1)}, u32[]{:S(2)}) copy-start(f32[512,128]{1,0:T(8,128)S(1)} %get-tuple-element.98) | copy-start | bytes 786436
  225.0 3.9 copy-start.17
  231.6 39.1 %copy-start.71 = (bf16[1024,16]{0,1:T(8,128)(2,1)S(1)}, bf16[1024,16]{0,1:T(8,128)(2,1)}, u32[]{:S(2)}) copy-start(bf16[1024,16]{0,1:T(8,128)(2,1)} %param.30) | copy-start | bytes 98308
  270.7 3.5 copy-start.59
  270.7 3.5 copy-start.28
  270.7 3.5 copy-start.55
  270.7 3.8 copy-start.67
  270.7 3.8 copy-start.73
  270.7 3.8 copy-start.58
  275.2 198.8 %all-reduce.23.cloned.1.call-start = ((), (), s32[]{:S(2)}) async-start(), calls=%async_computation.3 | async-start | bytes 12845056 | tf_op jit(solution)/shard_map/psum | solution.py:225
  474.1 5.9 %copy-start.45 = (bf16[1024,256]{1,0:T(8,128)(2,1)S(1)}, bf16[1024,256]{1,0:T(8,128)(2,1)}, u32[]{:S(2)}) copy-start(bf16[1024,256]{1,0:T(8,128)(2,1)} %get-tuple-element.88) | copy-start | bytes 1572868
  475.9 5.1 %copy-start.44 = (bf16[256,1024]{1,0:T(8,128)(2,1)S(1)}, bf16[256,1024]{1,0:T(8,128)(2,1)}, u32[]{:S(2)}) copy-start(bf16[256,1024]{1,0:T(8,128)(2,1)} %get-tuple-element.89) | copy-start | bytes 1572868
  477.7 4.3 copy-start.32
  (38 other events, 59.2 us)
Sparse Core Ops, SparseCore 0:
  45.5 54.1 all-reduce.16
  111.7 52.5 all-reduce.18
  201.6 69.1 all-reduce.24
  275.3 51.6 all-reduce.20
  331.5 142.4 all-reduce.22

commit v2 on v1

--- a/solution.py
+++ b/solution.py
@@ -1,3 +1,4 @@
+import functools
 import jax
 import jax.numpy as jnp
 import numpy as np
@@ -219,6 +220,125 @@
 
 def feed_piece(gate_pre, lift_pre):
     return jax.nn.silu(gate_pre) * lift_pre
+
+
+def peers_of(axes, sizes):
+    index = lax.axis_index(axes[0])
+    total = sizes[0]
+    for axis, size in zip(axes[1:], sizes[1:]):
+        index = index * size + lax.axis_index(axis)
+        total = total * size
+
+    def place(which):
+        coords = {}
+        for axis, size in reversed(list(zip(axes, sizes))):
+            coords[axis] = lax.rem(which, size)
+            which = which // size
+        return coords
+
+    others = [lax.rem(index + d, total) for d in range(1, total)]
+    return index, [(other, place(other)) for other in others]
+
+
+def greet(others):
+    barrier = pltpu.get_barrier_semaphore()
+    for _, place in others:
+        pl.semaphore_signal(barrier, inc=1, device_id=place, device_id_type=pl.DeviceIdType.MESH)
+    pl.semaphore_wait(barrier, len(others))
+
+
+def remote(src, dst, send, recv, place):
+    return pltpu.make_async_remote_copy(
+        src_ref=src, dst_ref=dst, send_sem=send, recv_sem=recv,
+        device_id=place, device_id_type=pl.DeviceIdType.MESH,
+    )
+
+
+def gather_kernel(axes, sizes, count, *refs):
+    arrays, outs = refs[:count], refs[count : 2 * count]
+    send, recv = refs[2 * count :]
+    me, others = peers_of(axes, sizes)
+    greet(others)
+    copies = []
+    for d, (_, place) in enumerate(others):
+        for a in range(count):
+            copies.append(remote(arrays[a], outs[a].at[me], send.at[a, d], recv.at[a, d], place))
+            copies[-1].start()
+    for a in range(count):
+        outs[a][me] = arrays[a][...]
+    for copy in copies:
+        copy.wait()
+
+
+def gather_direct(arrays, axes, sizes, ident):
+    total = int(np.prod(sizes))
+    vmem = pl.BlockSpec(memory_space=pltpu.VMEM)
+    return pl.pallas_call(
+        functools.partial(gather_kernel, axes, sizes, len(arrays)),
+        out_shape=[jax.ShapeDtypeStruct((total,) + a.shape, a.dtype) for a in arrays],
+        in_specs=[vmem] * len(arrays),
+        out_specs=[vmem] * len(arrays),
+        scratch_shapes=[pltpu.SemaphoreType.DMA((len(arrays), total - 1))] * 2,
+        compiler_params=pltpu.CompilerParams(
+            collective_id=ident, has_side_effects=True, vmem_limit_bytes=32 * 1024 * 1024
+        ),
+        cost_estimate=pl.CostEstimate(flops=0, bytes_accessed=12000000, transcendentals=0),
+    )(*arrays)
+
+
+def reduce_kernel(axes, sizes, count, *refs):
+    arrays, outs, lands = refs[:count], refs[count : 2 * count], refs[2 * count : 3 * count]
+    send_a, recv_a, send_b, recv_b = refs[3 * count :]
+    me, others = peers_of(axes, sizes)
+    total = len(others) + 1
+    greet(others)
+
+    def part(ref, which):
+        rows = ref.shape[0] // total
+        return ref.at[pl.ds(pl.multiple_of(which * rows, 16), rows)]
+
+    first = [[] for _ in range(count)]
+    for a in range(count):
+        for d, (other, place) in enumerate(others):
+            copy = remote(part(arrays[a], other), lands[a].at[d], send_a.at[a, d], recv_a.at[a, d], place)
+            copy.start()
+            first[a].append(copy)
+    second = []
+    for a in range(count):
+        value = part(arrays[a], me)[...].astype(jnp.float32)
+        for d in range(total - 1):
+            first[a][d].wait_recv()
+            value = value + lands[a][d].astype(jnp.float32)
+        part(outs[a], me)[...] = value.astype(outs[a].dtype)
+        for d, (_, place) in enumerate(others):
+            copy = remote(part(outs[a], me), part(outs[a], me), send_b.at[a, d], recv_b.at[a, d], place)
+            copy.start()
+            second.append(copy)
+    for a in range(count):
+        for copy in first[a]:
+            copy.wait_send()
+    for copy in second:
+        copy.wait()
+
+
+def reduce_direct(arrays, axes, sizes, ident):
+    total = int(np.prod(sizes))
+    vmem = pl.BlockSpec(memory_space=pltpu.VMEM)
+    count = len(arrays)
+    return pl.pallas_call(
+        functools.partial(reduce_kernel, axes, sizes, count),
+        out_shape=[jax.ShapeDtypeStruct(a.shape, a.dtype) for a in arrays],
+        in_specs=[vmem] * count,
+        out_specs=[vmem] * count,
+        scratch_shapes=[
+            pltpu.VMEM((total - 1, a.shape[0] // total, a.shape[1]), a.dtype) for a in arrays
+        ]
+        + [pltpu.SemaphoreType.DMA((count, total - 1))] * 4,
+        compiler_params=pltpu.CompilerParams(
+            collective_id=ident, has_side_effects=True, vmem_limit_bytes=32 * 1024 * 1024
+        ),
+        cost_estimate=pl.CostEstimate(flops=0, bytes_accessed=60000000 * count, transcendentals=0),
+    )(*arrays)
 
 
 def split_sum(grads):
@@ -294,15 +414,15 @@
         ),
         flops,
     )
+    tensor_size = lax.axis_size("tensor")
     seq_size = lax.axis_size("seq")
     seq_me = lax.axis_index("seq")
-    gathered = lax.all_gather(
-        jnp.concatenate([local_state, offsets[:, count]], 1), "seq"
-    )
-    totals = gathered[:, :, head_value : head_value + 1]
-    incoming = state_chain(
-        gathered[:, :, :head_value], totals, list(range(seq_size)), seq_me
-    )
+    flat_state = local_state.astype(jnp.bfloat16).reshape(groups * head_value, HEAD_KEY)
+    flat_total = offsets[:, count].reshape(groups * 8, HEAD_KEY)
+    gathered, totals = gather_direct((flat_state, flat_total), ("seq",), (seq_size,), 1)
+    gathered = gathered.reshape(seq_size, groups, head_value, HEAD_KEY).astype(jnp.float32)
+    totals = totals.reshape(seq_size, groups, 8, HEAD_KEY)[:, :, :1]
+    incoming = state_chain(gathered, totals, list(range(seq_size)), seq_me)
     recurrent = local_out + jnp.einsum(
         "ntd,ned->nte", decayed_q.astype(jnp.bfloat16), incoming.astype(jnp.bfloat16),
         preferred_element_type=jnp.float32,
@@ -314,7 +434,9 @@
     gated_f, head_back = jax.vjp(head_piece, recurrent, swish_gate, head_gain.astype(jnp.float32))
     gated = gated_f.astype(jnp.bfloat16).reshape(rows, value_width)
     mixer_part = jnp.dot(gated, output_proj, preferred_element_type=jnp.float32)
-    middle_own = inputs_flat + lax.psum(mixer_part.astype(jnp.bfloat16), "tensor").astype(jnp.float32)
+    middle_own = inputs_flat + reduce_direct(
+        (mixer_part.astype(jnp.bfloat16),), ("tensor",), (tensor_size,), 3
+    )[0].astype(jnp.float32)
     hidden_two_own, norm_two_back = jax.vjp(root_norm, middle_own, feed_gain_f)
     hidden_two = hidden_two_own.astype(jnp.bfloat16)
     gate_pre = jnp.dot(hidden_two, feed_gate, preferred_element_type=jnp.float32)
@@ -322,10 +444,6 @@
     activation_f, feed_back = jax.vjp(feed_piece, gate_pre, lift_pre)
     activation = activation_f.astype(jnp.bfloat16)
     feed_part = jnp.dot(activation, feed_down, preferred_element_type=jnp.float32)
-    mixed = (
-        middle_own + lax.psum(feed_part.astype(jnp.bfloat16), "tensor").astype(jnp.float32)
-    ).astype(jnp.bfloat16)
-    mixed = mixed.reshape(batch, seglen, width)
     upstream = cotangent.astype(jnp.float32).reshape(rows, width)
     feed_out_grad = cotangent.reshape(rows, width)
     grad_feed_down = jnp.dot(activation.T, feed_out_grad, preferred_element_type=jnp.float32)
@@ -338,7 +456,12 @@
     hidden_two_part = jnp.dot(
         gate_pre_grad, feed_gate.T, preferred_element_type=jnp.float32
     ) + jnp.dot(lift_pre_grad, feed_lift.T, preferred_element_type=jnp.float32)
-    two_grad_own = lax.psum(hidden_two_part.astype(jnp.bfloat16), "tensor").astype(jnp.float32)
+    grad_feed_gate, grad_feed_lift, grad_feed_down = split_sum(
+        (grad_feed_gate, grad_feed_lift, grad_feed_down)
+    )
+    two_grad_own = reduce_direct(
+        (hidden_two_part.astype(jnp.bfloat16),), ("tensor",), (tensor_size,), 4
+    )[0].astype(jnp.float32)
     middle_norm_grad, grad_feed_gain = norm_two_back(two_grad_own)
     middle_grad_own = upstream + middle_norm_grad
     mixer_grad = middle_grad_own.astype(jnp.bfloat16)
@@ -353,7 +476,9 @@
         "ntd,nte->ned", decayed_q.astype(jnp.bfloat16), recurrent_grad.astype(jnp.bfloat16),
         preferred_element_type=jnp.float32,
     )
-    pulls = lax.all_gather(local_pull.astype(jnp.bfloat16), "seq").astype(jnp.float32)
+    flat_pull = local_pull.astype(jnp.bfloat16).reshape(groups * head_value, HEAD_KEY)
+    (pulls,) = gather_direct((flat_pull,), ("seq",), (seq_size,), 2)
+    pulls = pulls.reshape(seq_size, groups, head_value, HEAD_KEY).astype(jnp.float32)
     outgoing_grad = state_chain(pulls, totals, list(range(seq_size))[::-1], seq_me)
     queries_grad, keys_grad, values_grad, decays_grad = run_groups(
         backward_kernel,
@@ -407,25 +532,44 @@
         + jnp.dot(swish_gate_grad, swish_proj.T, preferred_element_type=jnp.float32)
     )
     decay_down_f = decay_down.astype(jnp.float32)
-    hidden_sum, low_rank_grad, grad_head_gain = (
-        lax.psum(hidden_part.astype(jnp.bfloat16), "tensor").astype(jnp.float32),
-        lax.psum(low_rank_part.astype(jnp.bfloat16), "tensor").astype(jnp.float32),
-        lax.psum(head_gain_part.astype(jnp.bfloat16), "tensor").astype(jnp.float32),
-    )
-    hidden_grad = hidden_sum + jnp.dot(low_rank_grad, decay_down_f.T, precision=highest)
-    grad_decay_down = jnp.dot(hidden.astype(jnp.float32).T, low_rank_grad, precision=highest)
+    hidden_part = hidden_part + jnp.dot(low_rank_part, decay_down_f.T)
+    decay_down_part = lax.dot_general(low_rank_part, hidden.astype(jnp.float32), (((0,), (0,)), ((), ())))
+    rank = decay_down.shape[1]
+    spare = 16 * tensor_size - rank - 1
+    small_part = jnp.concatenate(
+        [
+            decay_down_part,
+            jnp.pad(head_gain_part, (0, width - head_value))[None],
+            jnp.zeros((spare, width), jnp.float32),
+        ],
+        0,
+    )
+    late = (grad_query_proj, grad_key_proj, grad_value_proj, grad_swish_proj, grad_output_proj)
+    late, grad_feed_gate, grad_feed_lift, grad_feed_down = lax.optimization_barrier(
+        (late, grad_feed_gate, grad_feed_lift, grad_feed_down)
+    )
+    grad_query_proj, grad_key_proj, grad_value_proj, grad_swish_proj, grad_output_proj = split_sum(late)
+    hidden_sum, feed_sum, small_sum = reduce_direct(
+        (
+            hidden_part.astype(jnp.bfloat16),
+            feed_part.astype(jnp.bfloat16),
+            small_part.astype(jnp.bfloat16),
+        ),
+        ("tensor",),
+        (tensor_size,),
+        5,
+    )
+    hidden_grad = hidden_sum.astype(jnp.float32)
+    mixed = (middle_own + feed_sum.astype(jnp.float32)).astype(jnp.bfloat16)
+    mixed = mixed.reshape(batch, seglen, width)
+    grad_decay_down = small_sum[:rank].astype(jnp.float32)
+    grad_head_gain = small_sum[rank, :head_value].astype(jnp.float32)
     inputs_norm_grad, grad_attention_gain = norm_back(hidden_grad)
     tokens_grad = middle_grad_own + inputs_norm_grad
     tokens_grad = tokens_grad.reshape(batch, seglen, width)
     grad_query_conv = conv_grad[:, :key_width]
     grad_key_conv = conv_grad[:, key_width : 2 * key_width]
     grad_value_conv = conv_grad[:, 2 * key_width :]
-    grad_query_proj, grad_key_proj, grad_value_proj, grad_swish_proj = split_sum(
-        (grad_query_proj, grad_key_proj, grad_value_proj, grad_swish_proj)
-    )
-    (grad_output_proj,) = split_sum((grad_output_proj,))
-    grad_feed_gate, grad_feed_lift = split_sum((grad_feed_gate, grad_feed_lift))
-    (grad_feed_down,) = split_sum((grad_feed_down,))
     small = (
         grad_attention_gain,
         grad_query_conv,
@@ -437,7 +581,11 @@
         grad_head_gain,
         grad_feed_gain,
     )
-    flat = lax.psum(jnp.concatenate([x.reshape(-1) for x in small]), ("dp", "seq"))
+    flat = jnp.concatenate([x.reshape(-1).astype(jnp.bfloat16) for x in small])
+    lines = -(-flat.size // (16 * width)) * 16
+    flat = jnp.pad(flat, (0, lines * width - flat.size)).reshape(lines, width)
+    (flat,) = gather_direct((flat,), ("dp", "seq"), (lax.axis_size("dp"), seq_size), 6)
+    flat = jnp.sum(flat.astype(jnp.float32), axis=0).reshape(-1)
     summed, start = [], 0
     for x in small:
         summed.append(flat[start : start + x.size].reshape(x.shape))
@@ -453,6 +601,7 @@
         grad_head_gain,
         grad_feed_gain,
     ) = summed
+    grad_decay_down = grad_decay_down.T
     return (
         mixed,
         tokens_grad,

time: 495 us -> 340 us (0.69)
  waiting for transfers between devices: 322 us -> 67.5 us
  Pallas kernels: 6.33 us -> 149 us
  blocking collectives: 46.6 us -> 0 us
  local copies, waits for them, and re-layouts: 19.7 us -> 30.6 us
  matrix products: 42.2 us -> 34.7 us
    psum x4 -> x0, waiting for transfers between devices: 180 us -> none  [the longest x1 54 us: on_device(): lax.psum(mixer_part.astype(jnp.bfloat16), 'tensor').astype(jnp.float32)]
    pallas_call x0 -> x6, Pallas kernels: none -> 143 us  [the longest x3 97.7 us: reduce_direct(): pl.pallas_call(functools.partial(reduce_kernel, axes, sizes, count), out_...]
    psum x1 -> x2, waiting for transfers between devices: 138 us -> 67.4 us  [split_sum(): lax.psum(tuple((g.astype(jnp.bfloat16) for g in grads)), ('dp', 'seq'))]
    all_gather x2 -> x0, blocking collectives: 30.2 us -> none  [the longest x1 16.1 us: on_device(): lax.all_gather(jnp.concatenate([local_state, offsets[:, count]], 1), 'seq')]
    psum x1 -> x0, blocking collectives: 16.3 us -> none  [on_device(): lax.psum(low_rank_part.astype(jnp.bfloat16), 'tensor').astype(jnp.float32)]
    unnamed x164 -> x163, local copies, waits for them, and re-layouts: 10.1 us -> 18.4 us
  transfers between devices with their start and end apart: 7 -> 4, of which waited for: 7 -> 2; matrix products, arithmetic and copies ran while one was open for 8% -> 12% of each run, Pallas kernels for 0% -> 21%
where the time goes in v2:
time: 340 us; the launch traced here: 339 us
  Pallas kernels  149 us (44%)
  waiting for transfers between devices  67.5 us (20%)
  other arithmetic  35.2 us (10%)
  matrix products  34.7 us (10%)
  local copies, waits for them, and re-layouts  30.6 us (9%)
  between operations  15.1 us (4%)
  starting transfers between devices  6.77 us (2%)
    pallas_call x3, Pallas kernels, reduce_direct(): pl.pallas_call(functools.partial(reduce_kernel, axes, sizes, count), out_...  97.7 us
    psum x2, waiting for transfers between devices, split_sum(): lax.psum(tuple((g.astype(jnp.bfloat16) for g in grads)), ('dp', 'seq'))  67.4 us
    pallas_call x3, Pallas kernels, gather_direct(): pl.pallas_call(functools.partial(gather_kernel, axes, sizes, len(arrays))...  45.1 us
    unnamed x163, local copies, waits for them, and re-layouts  18.4 us
    convert_element_type x8, other arithmetic, split_sum(): return tuple((g.astype(jnp.float32) for g in sums))  15.3 us
  transfers between devices with their start and end apart: 4, of which 2 were waited for; matrix products, arithmetic and copies ran while one was open for 12% of the time, Pallas kernels for 21%

profile of v2, /device:TPU:0, one launch (start us, length us, event | category | flops | bytes accessed | tf_op | source)
XLA Modules:
  0.0 339.0 jit_solution(6645547235334824794)
XLA Ops:
  8.1 1.5 fusion.11
  9.6 1.6 fusion.10
  12.9 5.1 %collective-permute-start = (bf16[1,3,512]{2,1,0:T(4,128)(2,1)S(1)}, bf16[1,3,512]{2,1,0:T(4,128)(2,1)S(1)}, u32[]{:S(2)}, u32[]{:S(2)}) collective-permute-start(bf16[1,3,512]{2,1,0:T(4,128)(2,1)S(1)} %slice.217), channel_id=1, source_target_pairs={{0,4},{4,8},{8,12},{1,5},{5,9},{9,13},{2,6},{6,10},{10,14},{3,7},{... | collective-permute-start | bytes 9224 | tf_op jit(solution)/shard_map/ppermute | solution.py:21
  19.7 2.0 fusion.34
  24.2 2.2 shard_map.348
  26.5 8.5 %shard_map.349 = (bf16[4,256,128]{2,1,0:T(8,128)(2,1)S(1)}, f32[4,8,128]{2,1,0:T(8,128)S(1)}) custom-call(bf16[256,128]{1,0:T(8,128)(2,1)S(1)} %convert_bitcast_fusion.1.refs_0_, f32[8,128]{1,0:T(8,128)S(1)} %slice_bitcast_fusion.2.refs_1_), custom_call_target="tpu_custom_call" | custom-call | bytes 12000000 | tf_op jit(solution)/shard_map/pallas_call | solution.py:276
  37.0 23.7 %shard_map.350 = bf16[512,1024]{1,0:T(8,128)(2,1)S(1)} custom-call(bf16[512,1024]{1,0:T(8,128)(2,1)S(1)} %convolution_convert_fusion.4.refs_0_), custom_call_target="tpu_custom_call" | custom-call | bytes 60000000 | tf_op jit(solution)/shard_map/pallas_call | solution.py:328
  63.9 1.5 multiply_convert_fusion.1
  67.5 25.5 %shard_map.351 = bf16[512,1024]{1,0:T(8,128)(2,1)S(1)} custom-call(bf16[512,1024]{1,0:T(8,128)(2,1)S(1)} %add_convert_fusion.2.refs_0_), custom_call_target="tpu_custom_call" | custom-call | bytes 60000000 | tf_op jit(solution)/shard_map/pallas_call | solution.py:328
  93.0 1.5 fusion.15
  94.5 1.9 multiply_reduce_fusion.5
  97.2 13.2 %shard_map.352 = bf16[4,256,128]{2,1,0:T(8,128)(2,1)S(1)} custom-call(bf16[256,128]{1,0:T(8,128)(2,1)S(1)} %convolution_convert_fusion.8.refs_0_), custom_call_target="tpu_custom_call" | custom-call | bytes 12000000 | tf_op jit(solution)/shard_map/pallas_call | solution.py:276
  110.5 4.1 %shard_map.353 = (f32[1,512,128]{2,1,0:T(8,128)S(1)}, f32[1,512,128]{2,1,0:T(8,128)S(1)}, f32[1,512,256]{2,1,0:T(8,128)S(1)}, f32[1,512,128]{2,1,0:T(8,128)S(1)}) custom-call(bf16[1152,128]{1,0:T(8,128)(2,1)S(1)} %copy-done.4, bf16[128,1152]{1,0:T(8,128)(2,1)S(1)} %copy-done.5, f32[1,512,128]{2,1,0:T(8,128)S(1)} %get-tuple-element.98.q_ref, ...), custom_call_target="tpu_custom_call" | custom-call | flops 3072000000 | bytes 4000000 | tf_op jit(solution)/shard_map/pallas_call | solution.py:180
  118.1 1.3 pad_add_fusion
  119.4 1.8 fusion.102
  121.2 1.5 fusion.31
  122.7 1.9 fusion.44
  124.6 2.0 convolution_convert_fusion.1
  126.7 2.0 convolution_convert_fusion
  128.7 2.0 convolution_convert_fusion.3.refs_1_
  130.7 2.0 convolution_convert_fusion.2
  132.8 1.6 collective-permute-start.1
  134.4 2.0 fusion.42
  136.4 1.5 fusion.90
  145.5 48.5 %shard_map.354 = (bf16[512,1024]{1,0:T(8,128)(2,1)S(1)}, bf16[512,1024]{1,0:T(8,128)(2,1)S(1)}, bf16[64,1024]{1,0:T(8,128)(2,1)S(1)}) custom-call(bf16[512,1024]{1,0:T(8,128)(2,1)S(1)} %add_convert_fusion.1.refs_0_, bf16[512,1024]{1,0:T(8,128)(2,1)S(1)} %copy-done.3, bf16[64,1024]{1,0:T(8,128)(2,1)S(1)} %maximum_maximum_fusion.refs_2_), custom_call_target="tpu_custom_call" | custom-call | bytes 180000000 | tf_op jit(solution)/shard_map/pallas_call | solution.py:328
  195.1 1.5 fusion.16
  197.2 1.4 dynamic-update-slice.1
  198.6 1.4 dynamic-update-slice.2
  201.2 1.8 fusion.26
  203.0 1.4 dynamic-update-slice.6
  204.5 1.4 dynamic-update-slice.7
  205.9 1.4 dynamic-update-slice.8
  208.2 23.3 %shard_map.355 = bf16[8,32,1024]{2,1,0:T(8,128)(2,1)S(1)} custom-call(bf16[32,1024]{1,0:T(8,128)(2,1)S(1)} %reshape.635.refs_0_), custom_call_target="tpu_custom_call" | custom-call | bytes 12000000 | tf_op jit(solution)/shard_map/pallas_call | solution.py:276
  231.6 1.2 slice_reduce_fusion
  232.8 2.4 fusion.104
  235.2 1.2 fusion.105
  236.4 1.3 fusion.71
  237.7 12.6 %all-reduce.17.cloned.1.call-done = (bf16[1024,704]{0,1:T(8,128)(2,1)}, bf16[1024,704]{0,1:T(8,128)(2,1)}, bf16[704,1024]{1,0:T(8,128)(2,1)}) async-done(((bf16[1024,704]{0,1:T(8,128)(2,1)}, bf16[1024,704]{0,1:T(8,128)(2,1)}, bf16[704,1024]{1,0:T(8,128)(2,1)}), (bf16[1024,704]{0,1:T(8,128)(2,1)}, bf16[1024,704]{0,1:T(8,128)(2,1)}, bf16[704,1024]{1,0:T(8,128)(2,1)})) %all-reduce.17.cloned.1.call-update) | async-done | bytes 4325392 | tf_op jit(solution)/shard_map/psum | solution.py:345
  250.3 3.4 %convert_element_type.280 = f32[1024,704]{0,1:T(8,128)} convert(bf16[1024,704]{0,1:T(8,128)(2,1)} %get-tuple-element.78) | non-fusion elementwise | flops 720896 | bytes 4325376 | tf_op jit(solution)/shard_map/convert_element_type | solution.py:346
  253.7 1.9 convert_element_type.282
  255.7 1.9 convert_element_type.284
  261.2 1.3 reshape.636
  262.5 1.3 reshape.637
  265.0 4.3 %fusion.19 = (f32[1,512,1024]{2,1,0:T(8,128)}, bf16[1,512,1024]{2,1,0:T(8,128)(2,1)}) fusion(bf16[1,512,1024]{2,1,0:T(8,128)(2,1)} %param.21, bf16[512,1024]{1,0:T(8,128)(2,1)S(1)} %get-tuple-element.53, f32[512]{0:T(512)} %multiply_multiply_fusion, f32[1024]{0:T(1024)S(1)} %copy-done.42, f32[512]{0:T(512)S(1)} %copy-done.48, f32[512]{0:T(512)} %copy-done.55, ...), kind=kLoop, calls=%fused_computation.28 | loop fusion | flops 11010048 | bytes 9453568 | tf_op jit(solution)/shard_map/reshape | solution.py:569
  269.4 54.8 %all-reduce.15.cloned.1.call-done = (bf16[1024,128]{1,0:T(8,128)(2,1)}, bf16[1024,128]{1,0:T(8,128)(2,1)}, bf16[1024,256]{1,0:T(8,128)(2,1)}, bf16[1024,256]{1,0:T(8,128)(2,1)}, bf16[256,1024]{1,0:T(8,128)(2,1)}) async-done(((bf16[1024,128]{1,0:T(8,128)(2,1)}, bf16[1024,128]{1,0:T(8,128)(2,1)}, bf16[1024,256]{1,0:T(8,128)(2,1)}, bf16[1024,256]{1,0:T(8,128)(2,1)}, bf16[256,1024]{1,0:T(8,128)(2,1)}), ...) | async-done | bytes 2097168 | tf_op jit(solution)/shard_map/psum | solution.py:345
  324.2 1.8 convert_element_type.286
  326.0 1.8 convert_element_type.288
  327.8 2.2 convert_element_type.290
  (238 shorter events, 35.8 us)
Async XLA Ops:
  7.2 56.3 %copy-start = (bf16[1024,704]{0,1:T(8,128)(2,1)S(1)}, bf16[1024,704]{0,1:T(8,128)(2,1)}, u32[]{:S(2)}) copy-start(bf16[1024,704]{0,1:T(8,128)(2,1)} %param.38) | copy-start | bytes 4325380
  7.2 4.0 %copy-start.35 = (bf16[1024,256]{1,0:T(8,128)(2,1)S(1)}, bf16[1024,256]{1,0:T(8,128)(2,1)}, u32[]{:S(2)}) copy-start(bf16[1024,256]{1,0:T(8,128)(2,1)} %param.26) | copy-start | bytes 1572868
  7.2 243.1 %all-reduce.17.cloned.1.call-start = ((), (), s32[]{:S(2)}) async-start(), calls=%async_computation.1 | async-start | bytes 8650752 | tf_op jit(solution)/shard_map/psum | solution.py:345
  8.1 113.1 %copy-start.41 = (f32[1024]{0:T(1024)}, f32[1024]{0:T(1024)S(1)}, u32[]{:S(2)}) copy-start(f32[1024]{0:T(1024)S(1)} %convert_element_type.235) | copy-start | bytes 12292
  9.6 2.6 copy-start.51
  9.6 111.6 %copy-start.47 = (f32[512]{0:T(512)}, f32[512]{0:T(512)S(1)}, u32[]{:S(2)}) copy-start(f32[512]{0:T(512)S(1)} %fusion.76) | copy-start | bytes 6148
  11.2 6.8 %copy-start.8 = (bf16[512,1024]{1,0:T(8,128)(2,1)}, bf16[512,1024]{1,0:T(8,128)(2,1)S(1)}, u32[]{:S(2)}) copy-start(bf16[512,1024]{1,0:T(8,128)(2,1)S(1)} %fusion.10) | copy-start | bytes 3145732
  11.7 6.3 %copy-start.39 = (bf16[1024,16]{0,1:T(8,128)(2,1)S(1)}, bf16[1024,16]{0,1:T(8,128)(2,1)}, u32[]{:S(2)}) copy-start(bf16[1024,16]{0,1:T(8,128)(2,1)} %param.30) | copy-start | bytes 98308
  12.4 6.6 %copy-start.53 = (bf16[16,128]{1,0:T(8,128)(2,1)S(1)}, bf16[16,128]{1,0:T(8,128)(2,1)}, u32[]{:S(2)}) copy-start(bf16[16,128]{1,0:T(8,128)(2,1)} %param.31) | copy-start | bytes 12292
  12.4 6.6 %copy-start.66 = (f32[128]{0:T(128)S(1)}, f32[128]{0:T(128)}, u32[]{:S(2)}) copy-start(f32[128]{0:T(128)} %param.32) | copy-start | bytes 1540
  12.4 7.2 %copy-start.25 = (bf16[1,512,1024]{2,1,0:T(8,128)(2,1)S(1)}, bf16[1,512,1024]{2,1,0:T(8,128)(2,1)}, u32[]{:S(2)}) copy-start(bf16[1,512,1024]{2,1,0:T(8,128)(2,1)} %param.22) | copy-start | bytes 3145732
  12.4 7.2 %copy-start.70 = (bf16[704,1024]{1,0:T(8,128)(2,1)S(1)}, bf16[704,1024]{1,0:T(8,128)(2,1)}, u32[]{:S(2)}) copy-start(bf16[704,1024]{1,0:T(8,128)(2,1)} %param.39) | copy-start | bytes 4325380
  12.9 9.5 %collective-permute-start = (bf16[1,3,512]{2,1,0:T(4,128)(2,1)S(1)}, bf16[1,3,512]{2,1,0:T(4,128)(2,1)S(1)}, u32[]{:S(2)}, u32[]{:S(2)}) collective-permute-start(bf16[1,3,512]{2,1,0:T(4,128)(2,1)S(1)} %slice.217), channel_id=1, source_target_pairs={{0,4},{4,8},{8,12},{1,5},{5,9},{9,13},{2,6},{6,10},{10,14},{3,7},{... | collective-permute-start | bytes 9224 | tf_op jit(solution)/shard_map/ppermute | solution.py:21
  19.4 2.3 copy-start.20
  19.6 2.1 copy-start.62
  19.6 2.1 copy-start.72
  19.7 2.1 copy-start.61
  21.8 100.9 %copy-start.43 = (f32[1024]{0:T(1024)}, f32[1024]{0:T(1024)S(1)}, u32[]{:S(2)}) copy-start(f32[1024]{0:T(1024)S(1)} %convert_element_type.250) | copy-start | bytes 12292
  26.4 9.1 %copy-start.9 = (bf16[512,1024]{1,0:T(8,128)(2,1)S(1)}, bf16[512,1024]{1,0:T(8,128)(2,1)}, u32[]{:S(2)}) copy-start(bf16[512,1024]{1,0:T(8,128)(2,1)} %copy-done.8) | copy-start | bytes 3145732
  26.4 9.1 %copy-start.34 = (bf16[1024,256]{1,0:T(8,128)(2,1)S(1)}, bf16[1024,256]{1,0:T(8,128)(2,1)}, u32[]{:S(2)}) copy-start(bf16[1024,256]{1,0:T(8,128)(2,1)} %param.33) | copy-start | bytes 1572868
  36.1 24.7 %copy-start.6 = (bf16[1,512,1024]{2,1,0:T(8,128)(2,1)S(1)}, bf16[1,512,1024]{2,1,0:T(8,128)(2,1)}, u32[]{:S(2)}) copy-start(bf16[1,512,1024]{2,1,0:T(8,128)(2,1)} %param.21) | copy-start | bytes 3145732
  61.2 61.5 %copy-start.49 = (f32[512]{0:T(512)}, f32[512]{0:T(512)S(1)}, u32[]{:S(2)}) copy-start(f32[512]{0:T(512)S(1)} %fusion.78) | copy-start | bytes 6148
  94.5 28.2 %copy-start.55 = (f32[512]{0:T(512)}, f32[512]{0:T(512)S(1)}, u32[]{:S(2)}) copy-start(f32[512]{0:T(512)S(1)} %multiply_multiply_fusion.2) | copy-start | bytes 6148
  96.5 14.0 %copy-start.5 = (bf16[128,1152]{1,0:T(8,128)(2,1)S(1)}, bf16[128,1152]{1,0:T(8,128)(2,1)}, u32[]{:S(2)}) copy-start(bf16[128,1152]{1,0:T(8,128)(2,1)} %constant.59.clone.rowst_ref) | copy-start | bytes 884740
  130.7 7.2 %copy-start.54 = (bf16[16,128]{1,0:T(8,128)(2,1)S(1)}, bf16[16,128]{1,0:T(8,128)(2,1)}, u32[]{:S(2)}) copy-start(bf16[16,128]{1,0:T(8,128)(2,1)} %param.31) | copy-start | bytes 12292
  130.7 7.4 %copy-start.68 = (bf16[256]{0:T(256)(128)(2,1)S(1)}, bf16[256]{0:T(256)(128)(2,1)}, u32[]{:S(2)}) copy-start(bf16[256]{0:T(256)(128)(2,1)} %get-tuple-element.71) | copy-start | bytes 1540
  130.7 7.5 %copy-start.10 = (bf16[512,1024]{1,0:T(8,128)(2,1)S(1)}, bf16[512,1024]{1,0:T(8,128)(2,1)}, u32[]{:S(2)}) copy-start(bf16[512,1024]{1,0:T(8,128)(2,1)} %copy-done.8) | copy-start | bytes 3145732
  132.8 5.7 %copy-start.67 = (bf16[64]{0:T(256)(128)(2,1)S(1)}, bf16[64]{0:T(256)(128)(2,1)}, u32[]{:S(2)}) copy-start(bf16[64]{0:T(256)(128)(2,1)} %pad.45.clone) | copy-start | bytes 388
  132.8 7.0 %collective-permute-start.1 = (f32[1,3,512]{2,1,0:T(4,128)S(1)}, f32[1,3,512]{2,1,0:T(4,128)S(1)}, u32[]{:S(2)}, u32[]{:S(2)}) collective-permute-start(f32[1,3,512]{2,1,0:T(4,128)S(1)} %pad_add_fusion.1), channel_id=1, source_target_pairs={{4,0},{8,4},{12,8},{5,1},{9,5},{13,9},{6,2},{10,6},{14,10},{7,3},{... | collective-permute-start | bytes 18440 | tf_op jit(solution)/shard_map/ppermute | solution.py:21
  139.8 184.4 %all-reduce.15.cloned.1.call-start = ((), (), s32[]{:S(2)}) async-start(), calls=%async_computation | async-start | bytes 4194304 | tf_op jit(solution)/shard_map/psum | solution.py:345
  145.5 49.5 %copy-start.7 = (bf16[1,512,1024]{2,1,0:T(8,128)(2,1)S(1)}, bf16[1,512,1024]{2,1,0:T(8,128)(2,1)}, u32[]{:S(2)}) copy-start(bf16[1,512,1024]{2,1,0:T(8,128)(2,1)} %param.21) | copy-start | bytes 3145732
  145.5 49.5 %copy-start.42 = (f32[1024]{0:T(1024)S(1)}, f32[1024]{0:T(1024)}, u32[]{:S(2)}) copy-start(f32[1024]{0:T(1024)} %copy-done.41) | copy-start | bytes 12292
  145.5 49.5 %copy-start.48 = (f32[512]{0:T(512)S(1)}, f32[512]{0:T(512)}, u32[]{:S(2)}) copy-start(f32[512]{0:T(512)} %copy-done.47) | copy-start | bytes 6148
  145.5 54.5 %copy-start.57 = (bf16[1,2,4,128]{3,1,2,0:T(2,128)(2,1)S(1)}, bf16[1,2,4,128]{3,1,2,0:T(2,128)(2,1)}, u32[]{:S(2)}) copy-start(bf16[1,2,4,128]{3,1,2,0:T(2,128)(2,1)} %copy.48) | copy-start | bytes 6148
  195.0 2.2 copy-start.60
  195.0 3.6 %copy-start.59 = (bf16[512]{0:T(512)(128)(2,1)S(1)}, bf16[512]{0:T(512)(128)(2,1)}, u32[]{:S(2)}) copy-start(bf16[512]{0:T(512)(128)(2,1)} %get-tuple-element.111) | copy-start | bytes 3076
  195.0 6.2 %copy-start.38 = (f32[512,16]{0,1:T(8,128)S(1)}, f32[512,16]{0,1:T(8,128)}, u32[]{:S(2)}) copy-start(f32[512,16]{0,1:T(8,128)} %copy-done.37) | copy-start | bytes 98308
  195.0 8.0 %copy-start.63 = (bf16[128]{0:T(256)(128)(2,1)S(1)}, bf16[128]{0:T(256)(128)(2,1)}, u32[]{:S(2)}) copy-start(bf16[128]{0:T(256)(128)(2,1)} %get-tuple-element.81) | copy-start | bytes 772
  195.0 10.9 %copy-start.58 = (bf16[1024]{0:T(1024)(128)(2,1)S(1)}, bf16[1024]{0:T(1024)(128)(2,1)}, u32[]{:S(2)}) copy-start(bf16[1024]{0:T(1024)(128)(2,1)} %get-tuple-element.63) | copy-start | bytes 6148
  208.2 27.1 %copy-start.11 = (bf16[512,1024]{1,0:T(8,128)(2,1)S(1)}, bf16[512,1024]{1,0:T(8,128)(2,1)}, u32[]{:S(2)}) copy-start(bf16[512,1024]{1,0:T(8,128)(2,1)} %copy-done.8) | copy-start | bytes 3145732
  208.2 28.2 %copy-start.19 = (bf16[509,512]{1,0:T(8,128)(2,1)S(1)}, bf16[509,512]{1,0:T(8,128)(2,1)}, u32[]{:S(2)}) copy-start(bf16[509,512]{1,0:T(8,128)(2,1)} %fusion.42) | copy-start | bytes 1563652
  208.2 28.2 %copy-start.46 = (bf16[3,512]{1,0:T(4,128)(2,1)S(1)}, bf16[3,512]{1,0:T(4,128)(2,1)}, u32[]{:S(2)}) copy-start(bf16[3,512]{1,0:T(4,128)(2,1)} %copy-done.45) | copy-start | bytes 9220
  250.3 3.4 %copy-start.23 = (bf16[1024,704]{0,1:T(8,128)(2,1)S(1)}, bf16[1024,704]{0,1:T(8,128)(2,1)}, u32[]{:S(2)}) copy-start(bf16[1024,704]{0,1:T(8,128)(2,1)} %get-tuple-element.79) | copy-start | bytes 4325380
  257.6 7.4 %copy-start.44 = (f32[1024]{0:T(1024)S(1)}, f32[1024]{0:T(1024)}, u32[]{:S(2)}) copy-start(f32[1024]{0:T(1024)} %copy-done.43) | copy-start | bytes 12292
  257.6 7.4 %copy-start.50 = (f32[512]{0:T(512)S(1)}, f32[512]{0:T(512)}, u32[]{:S(2)}) copy-start(f32[512]{0:T(512)} %copy-done.49) | copy-start | bytes 6148
  324.2 5.9 %copy-start.33 = (bf16[1024,256]{1,0:T(8,128)(2,1)S(1)}, bf16[1024,256]{1,0:T(8,128)(2,1)}, u32[]{:S(2)}) copy-start(bf16[1024,256]{1,0:T(8,128)(2,1)} %get-tuple-element.76) | copy-start | bytes 1572868
  326.0 5.1 %copy-start.32 = (bf16[256,1024]{1,0:T(8,128)(2,1)S(1)}, bf16[256,1024]{1,0:T(8,128)(2,1)}, u32[]{:S(2)}) copy-start(bf16[256,1024]{1,0:T(8,128)(2,1)} %get-tuple-element.77) | copy-start | bytes 1572868
  327.8 4.3 %copy-start.1 = (bf16[1024,704]{0,1:T(8,128)(2,1)S(1)}, bf16[1024,704]{0,1:T(8,128)(2,1)}, u32[]{:S(2)}) copy-start(bf16[1024,704]{0,1:T(8,128)(2,1)} %param.38) | copy-start | bytes 4325380
  (32 other events, 45.0 us)
Sparse Core Ops, SparseCore 0:
  139.9 110.3 all-reduce.16
  257.8 66.3 all-reduce.14
